TPU v7x, 256 devices: a whole 4x4x8 slice. The times are simulated.
256 devices in a mesh: dom: 16 (over y, x), edge: 16 (over z, core).
Axes of the slice: x: 4, y: 4, z: 8, core: 2. Of those that a mesh axis runs over, the one named last changes fastest.
Arguments:
- src_table: float32 [400, 131072], P(None, ('dom', 'edge')), may hold values from -2.5 to 2.5
- src_state: float32 [131072], P(('dom', 'edge')), may hold values from 0.001 to 1
- dst_table: float32 [400, 131072], P(None, ('dom', 'edge')), may hold values from -2.5 to 2.5
- dst_state: float32 [131072], P(('dom', 'edge')), may hold values from 0.001 to 1
- relation: float32 [400, 16], replicated, may hold values from -4 to 4
- edge_src: int32 [1048576], P(('dom', 'edge')), may hold values from 0 to 511
- edge_dst: int32 [1048576], P(('dom', 'edge')), may hold values from 0 to 511
- edge_rel: int32 [1048576], P(('dom', 'edge')), may hold values from 0 to 15
- matching: int32 [16], replicated, may hold values from 0 to 15, as said below
- neg_rows: int32 [256, 16, 256], P(('dom', 'edge')), may hold values from 0 to 511
- quotas: int32 [256, 16], P(('dom', 'edge')), may hold values from 0 to 2, as said below
Outputs:
- src_out: float32 [400, 131072], P(None, ('dom', 'edge'))
- src_state_out: float32 [131072], P(('dom', 'edge'))
- dst_out: float32 [400, 131072], P(None, ('dom', 'edge'))
- dst_state_out: float32 [131072], P(('dom', 'edge'))
- relation_out: float32 [400, 16], replicated
Inputs may be any that keep to these rules, and one draw needn't show every extreme that they name: matching names every partition exactly once. `quotas`: each device's 16 entries sum to exactly 12; for each index of dom, one index of edge is given 2 blocks by every device of that index of dom.
All inputs are finite; a program needn't handle non-finite values.
Results may differ from a plain program's by a relative error of at most 0.0011.
Values may be sent and summed in bfloat16 or wider, within the bound.
A program may use at most 128 MiB of HBM per device.

v0:
```python
import math

import jax
import jax.numpy as jnp
from jax import lax
from jax.sharding import PartitionSpec as P

DIM = 400
NREL = 16
BLOCK = 128
QMAX = 2
QTOTAL = 12
NNEG = 1536
SLOTS = 256


learn_rate = 0.1
rel_rate = 0.02


def complex_product(one_side, other_side):
    half_dim = one_side.shape[0] // 2
    real_part = (
        one_side[:half_dim] * other_side[:half_dim] - one_side[half_dim:] * other_side[half_dim:]
    )
    imag_part = (
        one_side[:half_dim] * other_side[half_dim:] + one_side[half_dim:] * other_side[:half_dim]
    )
    return jnp.concatenate([real_part, imag_part], axis=0)


def conj_product(gradient, operand):
    half_dim = gradient.shape[0] // 2
    real_part = gradient[:half_dim] * operand[:half_dim] + gradient[half_dim:] * operand[half_dim:]
    imag_part = gradient[half_dim:] * operand[:half_dim] - gradient[:half_dim] * operand[half_dim:]
    return jnp.concatenate([real_part, imag_part], axis=0)


def block_plan(quota_row, edge_count):
    block_ends = jnp.cumsum(quota_row)
    starts = block_ends - quota_row
    positions = jnp.arange(QTOTAL, dtype=jnp.int32)
    owner_of = jnp.sum((block_ends[None, :] <= positions[:, None]).astype(jnp.int32), axis=1)
    matches = owner_of[:, None] == jnp.arange(edge_count, dtype=jnp.int32)[None, :]
    first_block = jnp.sum(jnp.where(matches, starts[None, :], 0), axis=1)
    return (owner_of, owner_of * QMAX + positions - first_block)


def adagrad(table_in, state_in, gradient):
    new_state = state_in + jnp.mean(gradient * gradient, axis=-2)
    return (table_in - learn_rate * gradient / jnp.sqrt(new_state)[..., None, :], new_state)


def shards(
    src_table,
    src_state,
    dst_table,
    dst_state,
    relation,
    edge_src,
    edge_dst,
    edge_rel,
    matching,
    neg_rows,
    quotas,
):
    edge_count = lax.axis_size("edge")
    row_count = src_table.shape[1]
    held_state = dst_state.reshape(1, row_count)
    partner = lax.dynamic_index_in_dim(matching, lax.axis_index("dom"), 0, False)
    pieces = (
        lax.all_gather(dst_table, "dom", axis=1, tiled=True),
        lax.all_gather(held_state, "dom", axis=1, tiled=True),
    )
    piece_cols = pieces[0].shape[1]
    offset = partner * row_count
    inside = jnp.logical_and(offset >= 0, offset < piece_cols)
    anchor = jnp.clip(offset, 0, piece_cols - row_count)
    table_part = lax.dynamic_slice_in_dim(pieces[0], anchor, row_count, 1)
    state_part = lax.dynamic_slice_in_dim(pieces[1], anchor, row_count, 1)
    part_table = jnp.where(inside, table_part, jnp.zeros_like(dst_table))
    part_state = jnp.where(inside, state_part, jnp.zeros_like(held_state))
    own_requests = neg_rows.reshape(edge_count, SLOTS)
    requested = lax.all_to_all(own_requests, "edge", split_axis=0, concat_axis=0, tiled=True)
    served = part_table.astype(jnp.bfloat16)[:, requested]
    fetched = lax.all_to_all(served, "edge", split_axis=1, concat_axis=1, tiled=True)
    owner_of, block_at = block_plan(quotas.reshape(edge_count), edge_count)
    negatives = fetched.reshape(DIM, edge_count * QMAX, BLOCK)[:, block_at].reshape(DIM, NNEG)
    weight = 1.0 / math.sqrt(NNEG)
    labels = jnp.arange(NREL, dtype=jnp.int32)
    edge_total = edge_src.shape[0]
    edge_rows = min(edge_total, 512)
    groups = edge_total // edge_rows
    edge_sets = (
        edge_src.reshape(groups, edge_rows),
        edge_dst.reshape(groups, edge_rows),
        edge_rel.reshape(groups, edge_rows),
    )

    def edge_block(totals, pieces):
        src_grad, dst_grad, neg_grad, rel_grad = totals
        src_ids, dst_ids, rel_ids = pieces
        onehot = (rel_ids[None, :] == labels[:, None]).astype(jnp.float32)
        rel_edges = jnp.dot(relation, onehot, precision=lax.Precision.HIGHEST)
        src_rows = src_table[:, src_ids]
        dst_rows = part_table[:, dst_ids]
        queries = complex_product(src_rows, rel_edges)
        positive = jnp.sum(queries * dst_rows, axis=0)
        pos_coef = -jax.nn.sigmoid(-positive)
        query_b = queries.astype(jnp.bfloat16)
        scores = lax.dot_general(
            query_b, negatives, (((0,), (0,)), ((), ())), preferred_element_type=jnp.float32
        )
        neg_coef = (weight * jax.nn.sigmoid(scores)).astype(jnp.bfloat16)
        neg_grad = neg_grad + jnp.dot(query_b, neg_coef, preferred_element_type=jnp.float32)
        query_grad = pos_coef[None, :] * dst_rows + lax.dot_general(
            negatives, neg_coef, (((1,), (1,)), ((), ())), preferred_element_type=jnp.float32
        )
        src_grad = src_grad.at[:, src_ids].add(conj_product(query_grad, rel_edges))
        dst_grad = dst_grad.at[:, dst_ids].add(pos_coef[None, :] * queries)
        rel_grad = rel_grad + jnp.dot(
            conj_product(query_grad, src_rows), onehot.T, precision=lax.Precision.HIGHEST
        )
        return ((src_grad, dst_grad, neg_grad, rel_grad), None)

    start_totals = (
        jnp.zeros((DIM, row_count), jnp.float32),
        jnp.zeros((DIM, row_count), jnp.float32),
        jnp.zeros((DIM, NNEG), jnp.float32),
        jnp.zeros((DIM, NREL), jnp.float32),
    )
    summed, unused_out = lax.scan(edge_block, start_totals, edge_sets)
    src_grad, dst_grad, neg_grad, rel_grad = summed
    live_rows = own_requests.reshape(edge_count * QMAX, BLOCK)[block_at]
    columns = (owner_of[:, None] * row_count + live_rows).reshape(NNEG)
    dense = jnp.zeros((DIM, edge_count * row_count), jnp.float32).at[:, columns].add(neg_grad)
    dst_grad = dst_grad + lax.psum_scatter(dense, "edge", scatter_dimension=1, tiled=True)
    rel_total = lax.psum(rel_grad, ("dom", "edge"))
    src_out, src_state_out = adagrad(src_table, src_state, src_grad)
    dst_out, dst_state_new = adagrad(part_table, part_state.reshape(row_count), dst_grad)
    relation_out = relation - rel_rate * rel_total
    return (src_out, src_state_out, dst_out, dst_state_new, relation_out)


def solution(mesh):
    in_specs = (
        P(None, ("dom", "edge")),
        P(("dom", "edge")),
        P(None, ("dom", "edge")),
        P(("dom", "edge")),
        P(),
        P(("dom", "edge")),
        P(("dom", "edge")),
        P(("dom", "edge")),
        P(),
        P(("dom", "edge"), None, None),
        P(("dom", "edge"), None),
    )
    out_specs = (
        P(None, ("dom", "edge")),
        P(("dom", "edge")),
        P(None, ("dom", "edge")),
        P(("dom", "edge")),
        P(),
    )
    return jax.shard_map(shards, mesh=mesh, in_specs=in_specs, out_specs=out_specs, check_vma=False)
```

profile of v0, /device:TPU:1, one launch (start us, length us, event | category | flops | bytes accessed | tf_op | source)
XLA Modules:
  0.0 789.2 jit_solution(10643486582579046948)
XLA Ops:
  10.4 10.0 %all-to-all-start = ((s32[16,1,256]{2,1,0:T(1,128)}), s32[16,1,256]{2,1,0:T(1,128)S(1)}, u32[]{:S(2)}, u32[]{:S(2)}) async-start(s32[16,1,256]{2,1,0:T(1,128)} %all_to_all.11), calls=%async_computation | async-start | bytes 32768 | tf_op jit(solution)/shard_map/all_to_all | solution.py:84
  21.6 6.1 all-to-all-done
  27.7 102.9 %all-gather.4.cloned.1.call-done = f32[400,8192]{0,1:T(8,128)} async-done(((f32[400,512]{0,1:T(8,128)}), f32[400,8192]{0,1:T(8,128)}) %all-gather.4.cloned.1.call-update) | async-done | bytes 13107216 | tf_op jit(solution)/shard_map/all_gather | solution.py:72
  132.0 17.3 %gather_fusion.2 = bf16[4096,400]{1,0:T(8,128)(2,1)} fusion(bf16[400,512]{0,1:T(8,128)(2,1)S(1)} %get-tuple-element.233, s32[4096]{0:T(1024)S(1)} %broadcast_clamp_fusion), kind=kCustom, calls=%fused_computation.2 | custom fusion | bytes 6569984 | tf_op jit(solution)/shard_map/gather | solution.py:85
  149.4 6.1 copy.73
  155.4 7.9 all-to-all-start.1
  167.8 69.5 %all-to-all-done.1 = bf16[400,16,256]{2,0,1:T(8,128)(2,1)} async-done(((bf16[400,16,256]{2,0,1:T(8,128)(2,1)}), bf16[400,16,256]{2,0,1:T(8,128)(2,1)}, u32[]{:S(2)}, u32[]{:S(2)}) %all-to-all-start.1) | async-done | bytes 3276832 | tf_op jit(solution)/shard_map/all_to_all | solution.py:86
  237.3 4.8 copy.74
  242.0 6.0 reshape.228
  248.1 4.9 copy.76
  257.1 398.5 %while.17 = (s32[]{:T(128)}, f32[400,512]{0,1:T(8,128)S(1)}, f32[400,512]{0,1:T(8,128)S(1)}, f32[400,1536]{1,0:T(8,128)}, f32[400,16]{0,1:T(8,128)}, /*index=5*/...) while((s32[]{:T(128)}, f32[400,512]{0,1:T(8,128)S(1)}, ...), condition=%wide.region_7.8_spmd.clone, body=%wide.region_3.7_spmd.clone.sunk | while | flops 1977010688 | bytes 71210600 | solution.py:132
  259.2 3.9 gather_fusion
  289.7 4.6 scatter_fusion.1
  294.4 3.9 convolution_add_fusion.4
  301.7 4.7 scatter_fusion
  308.3 3.9 gather_fusion
  338.8 4.6 scatter_fusion.1
  343.5 4.7 convolution_add_fusion.4
  351.6 4.7 scatter_fusion
  358.2 3.9 gather_fusion
  388.7 4.6 scatter_fusion.1
  393.4 4.7 convolution_add_fusion.4
  401.5 4.7 scatter_fusion
  408.1 3.9 gather_fusion
  438.6 4.6 scatter_fusion.1
  443.3 4.7 convolution_add_fusion.4
  451.4 4.7 scatter_fusion
  458.0 3.9 gather_fusion
  488.5 4.6 scatter_fusion.1
  493.2 4.7 convolution_add_fusion.4
  501.2 4.7 scatter_fusion
  507.9 3.9 gather_fusion
  538.4 4.6 scatter_fusion.1
  543.0 4.7 convolution_add_fusion.4
  551.1 4.7 scatter_fusion
  557.8 3.9 gather_fusion
  588.3 4.6 scatter_fusion.1
  592.9 4.7 convolution_add_fusion.4
  601.0 4.7 scatter_fusion
  607.6 3.9 gather_fusion
  625.0 3.0 multiply_convert_fusion.2
  638.1 4.6 scatter_fusion.1
  642.8 4.7 convolution_add_fusion.4
  650.9 4.7 scatter_fusion
  655.6 3.4 copy.80
  659.0 17.0 %scatter_custom_fusion.2 = f32[400,8192]{0,1:T(8,128)} fusion(s32[1536]{0:T(1024)} %fusion.19, f32[1536,400]{1,0:T(8,128)} %copy.80, f32[]{:T(128)} %constant.31.clone.1), kind=kCustom, calls=%fused_computation.46 | custom fusion | flops 614400 | bytes 13107712 | tf_op jit(solution)/shard_map/scatter-add | solution.py:136
  676.7 18.6 %all-gather.1 = f32[16,1,512]{2,1,0:T(1,128)S(1)} all-gather(f32[1,1,512]{2,1,0:T(1,128)S(1)} %bitcast.114), channel_id=2, replica_groups=mesh['dom'=16,'edge'=16] {'dom'}, dimensions={0}, use_global_device_ids=true | all-gather | bytes 34816 | tf_op jit(solution)/shard_map/all_gather | solution.py:73
  695.3 79.7 %psum.7 = f32[400,16]{0,1:T(8,128)S(1)} all-reduce(f32[400,16]{0,1:T(8,128)S(1)} %copy-done.11), channel_id=1, replica_groups=mesh['dom'=16,'edge'=16] {'dom','edge'}, use_global_device_ids=true, to_apply=%region_12.13 | all-reduce | flops 6400 | bytes 51200 | tf_op jit(solution)/shard_map/psum | solution.py:138
  (479 shorter events, 272.8 us)
Async XLA Ops:
  7.2 13.2 %copy-start.30 = (s32[16]{0:T(128)S(1)}, s32[16]{0:T(128)}, u32[]{:S(2)}) copy-start(s32[16]{0:T(128)} %param.21) | copy-start | bytes 196
  7.2 123.4 %all-gather.4.cloned.1.call-start = ((), (), s32[]{:S(2)}) async-start(), calls=%async_computation.3 | async-start | bytes 17825792 | tf_op jit(solution)/shard_map/all_gather | solution.py:72
  10.4 17.3 %all-to-all-start = ((s32[16,1,256]{2,1,0:T(1,128)}), s32[16,1,256]{2,1,0:T(1,128)S(1)}, u32[]{:S(2)}, u32[]{:S(2)}) async-start(s32[16,1,256]{2,1,0:T(1,128)} %all_to_all.11), calls=%async_computation | async-start | bytes 32768 | tf_op jit(solution)/shard_map/all_to_all | solution.py:84
  155.4 8.0 %copy-start.29 = (s32[1,16]{1,0:T(1,128)S(1)}, s32[1,16]{1,0:T(1,128)}, u32[]{:S(2)}) copy-start(s32[1,16]{1,0:T(1,128)} %param.23) | copy-start | bytes 196
  155.4 8.2 %copy-start.15 = (f32[400,512]{1,0:T(8,128)S(1)}, f32[400,512]{1,0:T(8,128)}, u32[]{:S(2)}) copy-start(f32[400,512]{1,0:T(8,128)} %param.13) | copy-start | bytes 2457604
  155.4 9.6 %copy-start.24 = (s32[4096]{0:T(1024)S(1)}, s32[4096]{0:T(1024)}, u32[]{:S(2)}) copy-start(s32[4096]{0:T(1024)} %param.18) | copy-start | bytes 49156
  155.4 10.2 %copy-start.25 = (s32[4096]{0:T(1024)S(1)}, s32[4096]{0:T(1024)}, u32[]{:S(2)}) copy-start(s32[4096]{0:T(1024)} %param.20) | copy-start | bytes 49156
  155.4 10.2 %copy-start.26 = (s32[4096]{0:T(1024)S(1)}, s32[4096]{0:T(1024)}, u32[]{:S(2)}) copy-start(s32[4096]{0:T(1024)} %param.19) | copy-start | bytes 49156
  155.4 81.8 %all-to-all-start.1 = ((bf16[400,16,256]{2,0,1:T(8,128)(2,1)}), bf16[400,16,256]{2,0,1:T(8,128)(2,1)}, u32[]{:S(2)}, u32[]{:S(2)}) async-start(bf16[400,16,256]{2,0,1:T(8,128)(2,1)} %bitcast.105), calls=%async_computation.1 | async-start | bytes 6553600 | tf_op jit(solution)/shard_map/all_to_all | solution.py:86
  163.3 612.4 %reduce-scatter.2.cloned.1.call-start = ((), (), s32[]{:S(2)}) async-start(), calls=%async_computation.4 | async-start | bytes 17825792 | tf_op jit(solution)/shard_map/reduce_scatter | solution.py:137
  257.3 8.3 %copy-start.22 = (s32[8,512]{1,0:T(8,128)}, s32[8,512]{1,0:T(8,128)S(1)}, u32[]{:S(2)}) copy-start(s32[8,512]{1,0:T(8,128)S(1)} %get-tuple-element.371) | copy-start | bytes 49156 | tf_op jit(solution)/shard_map/while
  301.7 4.7 copy-start.13
  301.7 4.7 copy-start.23
  306.4 8.3 %copy-start.22 = (s32[8,512]{1,0:T(8,128)}, s32[8,512]{1,0:T(8,128)S(1)}, u32[]{:S(2)}) copy-start(s32[8,512]{1,0:T(8,128)S(1)} %get-tuple-element.371) | copy-start | bytes 49156 | tf_op jit(solution)/shard_map/while
  343.5 4.7 copy-start.5
  343.5 4.7 copy-start.6
  351.6 4.7 copy-start.13
  351.6 4.7 copy-start.23
  356.3 8.3 %copy-start.22 = (s32[8,512]{1,0:T(8,128)}, s32[8,512]{1,0:T(8,128)S(1)}, u32[]{:S(2)}) copy-start(s32[8,512]{1,0:T(8,128)S(1)} %get-tuple-element.371) | copy-start | bytes 49156 | tf_op jit(solution)/shard_map/while
  393.4 4.7 copy-start.5
  393.4 4.7 copy-start.6
  401.5 4.7 copy-start.13
  401.5 4.7 copy-start.23
  406.2 8.3 %copy-start.22 = (s32[8,512]{1,0:T(8,128)}, s32[8,512]{1,0:T(8,128)S(1)}, u32[]{:S(2)}) copy-start(s32[8,512]{1,0:T(8,128)S(1)} %get-tuple-element.371) | copy-start | bytes 49156 | tf_op jit(solution)/shard_map/while
  443.3 4.7 copy-start.5
  443.3 4.7 copy-start.6
  451.4 4.7 copy-start.13
  451.4 4.7 copy-start.23
  456.1 8.3 %copy-start.22 = (s32[8,512]{1,0:T(8,128)}, s32[8,512]{1,0:T(8,128)S(1)}, u32[]{:S(2)}) copy-start(s32[8,512]{1,0:T(8,128)S(1)} %get-tuple-element.371) | copy-start | bytes 49156 | tf_op jit(solution)/shard_map/while
  493.1 4.7 copy-start.5
  493.1 4.7 copy-start.6
  501.2 4.7 copy-start.13
  501.2 4.7 copy-start.23
  505.9 8.3 %copy-start.22 = (s32[8,512]{1,0:T(8,128)}, s32[8,512]{1,0:T(8,128)S(1)}, u32[]{:S(2)}) copy-start(s32[8,512]{1,0:T(8,128)S(1)} %get-tuple-element.371) | copy-start | bytes 49156 | tf_op jit(solution)/shard_map/while
  543.0 4.7 copy-start.5
  543.0 4.7 copy-start.6
  551.1 4.7 copy-start.23
  555.8 8.3 %copy-start.22 = (s32[8,512]{1,0:T(8,128)}, s32[8,512]{1,0:T(8,128)S(1)}, u32[]{:S(2)}) copy-start(s32[8,512]{1,0:T(8,128)S(1)} %get-tuple-element.371) | copy-start | bytes 49156 | tf_op jit(solution)/shard_map/while
  592.9 4.7 copy-start.5
  592.9 4.7 copy-start.6
  601.0 4.7 copy-start.13
  601.0 4.7 copy-start.23
  605.7 8.3 %copy-start.22 = (s32[8,512]{1,0:T(8,128)}, s32[8,512]{1,0:T(8,128)S(1)}, u32[]{:S(2)}) copy-start(s32[8,512]{1,0:T(8,128)S(1)} %get-tuple-element.371) | copy-start | bytes 49156 | tf_op jit(solution)/shard_map/while
  642.8 4.7 copy-start.5
  642.8 4.7 copy-start.6
  650.9 4.7 copy-start.23
  676.0 19.3 %copy-start.11 = (f32[400,16]{0,1:T(8,128)S(1)}, f32[400,16]{0,1:T(8,128)}, u32[]{:S(2)}) copy-start(f32[400,16]{0,1:T(8,128)} %get-tuple-element.393) | copy-start | bytes 76804
  676.0 99.0 %copy-start.14 = (f32[400,16]{0,1:T(8,128)S(1)}, f32[400,16]{0,1:T(8,128)}, u32[]{:S(2)}) copy-start(f32[400,16]{0,1:T(8,128)} %param.17) | copy-start | bytes 76804
  (99 other events, 217.3 us)
Sparse Core Ops, SparseCore 0:
  10.5 120.0 all-gather.3
  676.2 97.9 reduce-scatter.1
where the time goes:
time: 794 us; the launch traced here: 789 us
  local copies, waits for them, and re-layouts  211 us (27%)
  waiting for transfers between devices  178 us (22%)
  other arithmetic  177 us (22%)
  blocking collectives  98.4 us (12%)
  matrix products  89.6 us (11%)
  starting transfers between devices  18 us (2%)
  between operations  14.9 us (2%)
    all_gather x1, waiting for transfers between devices, shards(): lax.all_gather(dst_table, 'dom', axis=1, tiled=True)  103 us
    psum x1, blocking collectives, shards(): rel_total = lax.psum(rel_grad, ('dom', 'edge'))  79.7 us
    all_to_all x1, waiting for transfers between devices, shards(): lax.all_to_all(served, 'edge', split_axis=1, concat_axis=1, tiled=True)  69.5 us
    gather x16, local copies, waits for them, and re-layouts, edge_block(): src_rows = src_table[:, src_ids]  50.8 us
    gather x16, local copies, waits for them, and re-layouts, edge_block(): dst_rows = part_table[:, dst_ids]  38.9 us
    scatter-add x8, other arithmetic, edge_block(): src_grad = src_grad.at[:, src_ids].add(conj_product(query_grad, rel_edges))  37.2 us
    scatter-add x8, other arithmetic, edge_block(): dst_grad = dst_grad.at[:, dst_ids].add(pos_coef[None, :] * queries)  37.2 us
    dot_general x8, matrix products, edge_block(): jnp.dot(query_b, neg_coef, preferred_element_type=jnp.float32)  36.6 us
  transfers between devices with their start and end apart: 4, of which 3 were waited for; matrix products, arithmetic and copies ran while one was open for 1% of the time, Pallas kernels for 0%

commit v1 on v0

v1 whole, which is shorter than its diff:
```python
import math

import jax
import jax.numpy as jnp
from jax import lax
from jax.experimental import pallas as pl
from jax.experimental.pallas import tpu as pltpu
from jax.sharding import PartitionSpec as P

DIM = 400
HALF = 200
NREL = 16
BLOCK = 128
QMAX = 2
QTOTAL = 12
NNEG = 1536
ROWS = 512
EDGES = 4096
N_DOM = 16
N_EDGE = 16
N_Z = 8
FAR = N_Z // 2

PIECE_ROWS = 112
PIECE_COLS = 128
PAD_DIM = 448
CUT = ((0, 208), (208, 192))

CHUNK = 512
SLOT_COLS = NNEG + QMAX * BLOCK

learn_rate = 0.1
rel_rate = 0.02
weight = 1.0 / math.sqrt(NNEG)

F32 = jnp.float32
BF16 = jnp.bfloat16
VMEM = pltpu.VMEM
HBM = pl.ANY
SMEM = pltpu.SMEM
BY_COLS = (((1,), (1,)), ((), ()))


def on(p, e):
    return {"dom": p, "edge": e}


def remote(src, dst, send_sem, recv_sem, p, e):
    return pltpu.make_async_remote_copy(
        src_ref=src,
        dst_ref=dst,
        send_sem=send_sem,
        recv_sem=recv_sem,
        device_id=on(p, e),
        device_id_type=pl.DeviceIdType.MESH,
    )


def greet(devices):
    barrier = pltpu.get_barrier_semaphore()
    for p, e in devices:
        pl.semaphore_signal(
            barrier, inc=1, device_id=on(p, e), device_id_type=pl.DeviceIdType.MESH
        )
    pl.semaphore_wait(barrier, len(devices))


def split(x):
    high = x.astype(BF16)
    return high, (x - high.astype(F32)).astype(BF16)


def piece(k):
    rows = pl.ds(pl.multiple_of((k // 4) * PIECE_ROWS, 16), PIECE_ROWS)
    cols = pl.ds(pl.multiple_of((k % 4) * PIECE_COLS, 128), PIECE_COLS)
    return rows, cols


def pair_kernel(
    matching, table, state, shards_out, low_out, state_out,
    shards, low, own, landed_high, landed_low, picked, states,
    own_send, own_recv, pick_send, pick_recv, state_send, state_recv,
    right_send, right_recv, left_send, left_recv, core_send, core_recv, out_sem,
):
    p = lax.axis_index("dom")
    e = lax.axis_index("edge")
    z, core = e // 2, e % 2
    right = ((z + 1) % N_Z) * 2 + core
    left = ((z + N_Z - 1) % N_Z) * 2 + core
    sibling = z * 2 + 1 - core
    others = [(p + k) % N_DOM for k in range(1, N_DOM)]

    high_part, low_part = split(table[...])
    own[0, :DIM] = high_part
    own[1, :DIM] = low_part
    own[:, DIM:] = jnp.zeros((2, PAD_DIM - DIM, ROWS), BF16)
    states[p] = state[...]
    rows_p, cols_p = piece(p)

    greet([(t, e) for t in others] + [(p, right), (p, left), (p, sibling)])

    landed = (landed_high, landed_low)
    own_copies = [[], []]
    for part in range(2):
        for k, t in enumerate(others):
            rows, cols = piece(t)
            copy = remote(
                own.at[part, rows, cols], landed[part].at[p],
                own_send.at[part, k], own_recv.at[part, k], t, e,
            )
            copy.start()
            own_copies[part].append(copy)
        landed[part][p] = own[part, rows_p, cols_p]
    state_copies = []
    for k, t in enumerate(others):
        copy = remote(states.at[p], states.at[p], state_send.at[k], state_recv.at[k], t, e)
        copy.start()
        state_copies.append(copy)

    pick_copies = [[], []]

    def pick(part, target_ref):
        for copy in own_copies[part]:
            copy.wait_recv()
        for k, t in enumerate(others):
            picked[part, k] = landed[part][matching[t]]
            copy = remote(
                picked.at[part, k], target_ref.at[rows_p, cols_p],
                pick_send.at[part, k], pick_recv.at[part, k], t, e,
            )
            copy.start()
            pick_copies[part].append(copy)
        target_ref[rows_p, cols_p] = landed[part][matching[p]]

    pick(0, shards.at[e])
    pick(1, low)
    for copy in pick_copies[0]:
        copy.wait_recv()

    pending = []

    def go(step, half, to_right):
        source = ((z - step + N_Z) % N_Z if to_right else (z + step) % N_Z) * 2 + core
        start, size = CUT[half]
        ref = shards.at[source, pl.ds(start, size)]
        sems = (right_send, right_recv) if to_right else (left_send, left_recv)
        copy = remote(
            ref, ref, sems[0].at[step, half], sems[1].at[step, half],
            p, right if to_right else left,
        )
        copy.start()
        pending.append(copy)
        return copy

    across = []

    def cross(slot, source_z, half):
        start, size = CUT[half]
        ref = shards.at[source_z * 2 + core, pl.ds(start, size)]
        copy = remote(ref, ref, core_send.at[slot, half], core_recv.at[slot, half], p, sibling)
        copy.start()
        across.append(copy)

    flying = {}
    for half in range(2):
        flying[True, half] = go(0, half, True)
        flying[False, half] = go(0, half, False)
    for half in range(2):
        cross(0, z, half)
    for step in range(1, FAR + 1):
        for half in range(2):
            for to_right in (True, False):
                if step == FAR and to_right != (half == 0):
                    continue
                flying[to_right, half].wait_recv()
                source_z = (z - step + N_Z) % N_Z if to_right else (z + step) % N_Z
                if step < FAR - 1 or (step == FAR - 1 and to_right == (half == 0)):
                    flying[to_right, half] = go(step, half, to_right)
                if step == FAR:
                    slot = 2 * FAR - 1
                else:
                    slot = 2 * step - 1 if to_right else 2 * step
                cross(slot, source_z, half)

    for copy in own_copies[0] + own_copies[1] + pick_copies[0] + pending + across:
        copy.wait_send()
    for copy in pick_copies[1] + state_copies:
        copy.wait()
    for copy in across:
        copy.wait_recv()

    done = pltpu.make_async_copy(shards.at[:, pl.ds(0, DIM)], shards_out, out_sem.at[0])
    done.start()
    low_done = pltpu.make_async_copy(low.at[pl.ds(0, DIM)], low_out, out_sem.at[1])
    low_done.start()
    state_out[...] = states[matching[p]]
    done.wait()
    low_done.wait()


def pair(matching, table, state):
    dma = pltpu.SemaphoreType.DMA
    return pl.pallas_call(
        pair_kernel,
        out_shape=(
            jax.ShapeDtypeStruct((N_EDGE, DIM, ROWS), BF16),
            jax.ShapeDtypeStruct((DIM, ROWS), BF16),
            jax.ShapeDtypeStruct((1, ROWS), F32),
        ),
        in_specs=[
            pl.BlockSpec(memory_space=SMEM),
            pl.BlockSpec(memory_space=VMEM),
            pl.BlockSpec(memory_space=VMEM),
        ],
        out_specs=(
            pl.BlockSpec(memory_space=HBM),
            pl.BlockSpec(memory_space=HBM),
            pl.BlockSpec(memory_space=VMEM),
        ),
        scratch_shapes=[
            VMEM((N_EDGE, PAD_DIM, ROWS), BF16),
            VMEM((PAD_DIM, ROWS), BF16),
            VMEM((2, PAD_DIM, ROWS), BF16),
            VMEM((N_DOM, PIECE_ROWS, PIECE_COLS), BF16),
            VMEM((N_DOM, PIECE_ROWS, PIECE_COLS), BF16),
            VMEM((2, N_DOM - 1, PIECE_ROWS, PIECE_COLS), BF16),
            VMEM((N_DOM, 1, ROWS), F32),
            dma((2, N_DOM - 1)), dma((2, N_DOM - 1)),
            dma((2, N_DOM - 1)), dma((2, N_DOM - 1)),
            dma((N_DOM - 1,)), dma((N_DOM - 1,)),
            dma((FAR, 2)), dma((FAR, 2)), dma((FAR, 2)), dma((FAR, 2)),
            dma((N_Z, 2)), dma((N_Z, 2)),
            dma((2,)),
        ],
        compiler_params=pltpu.CompilerParams(
            collective_id=0, has_side_effects=True, vmem_limit_bytes=48 * 2**20
        ),
        name="pair_and_gather",
    )(matching, table, state)


def product(x_re, x_im, y_re, y_im):
    return x_re * y_re - x_im * y_im, x_re * y_im + x_im * y_re


def back(g_re, g_im, v_re, v_im):
    return g_re * v_re + g_im * v_im, g_im * v_re - g_re * v_im


def onehot(ids, count):
    places = lax.broadcasted_iota(jnp.int32, (count, ids.shape[1]), 0)
    return jnp.where(places == ids, 1.0, 0.0).astype(BF16)


def put_split(ref, re, im):
    x = jnp.concatenate([re, im], axis=0)
    high, low = split(x)
    ref[:DIM] = high
    ref[DIM:] = low


def both(x):
    return x[:HALF] + x[DIM : DIM + HALF], x[HALF:DIM] + x[DIM + HALF :]


def step_kernel(
    quotas, table, shards, low, relation, src_ids, dst_ids, rel_ids, neg_ids,
    dense_out, dst_out, src_out, rel_out,
    table2, part2, rel2, negs, negs_t, neg_grad, spread, src_acc, dst_acc, rel_acc,
):
    e = lax.axis_index("edge")
    ends = []
    total = 0
    for k in range(N_EDGE):
        total = total + quotas[0, k]
        ends.append(total)
    for j in range(QTOTAL):
        owner = 0
        for k in range(N_EDGE):
            owner = owner + jnp.where(ends[k] <= j, 1, 0)
        owner = jnp.minimum(owner, N_EDGE - 1)
        first = 0
        for k in range(N_EDGE):
            first = first + jnp.where(owner == k, ends[k] - quotas[0, k], 0)
        block = jnp.clip(owner * QMAX + j - first, 0, N_EDGE * QMAX - 1)
        rows = neg_ids[pl.ds(block, 1), :]
        found = jnp.dot(shards[owner], onehot(rows, ROWS), preferred_element_type=F32)
        negs[:, j * BLOCK : (j + 1) * BLOCK] = found.astype(BF16)
        negs_t[j * BLOCK : (j + 1) * BLOCK, :] = found.T.astype(BF16)

    table2[:DIM], table2[DIM:] = split(table[...])
    part2[:DIM] = shards[e]
    part2[DIM:] = low[...]
    rel2[:DIM], rel2[DIM:] = split(relation[...])
    neg_grad[...] = jnp.zeros_like(neg_grad)
    src_acc[...] = jnp.zeros_like(src_acc)
    dst_acc[...] = jnp.zeros_like(dst_acc)
    rel_acc[...] = jnp.zeros_like(rel_acc)

    @pl.loop(0, EDGES // CHUNK)
    def _(i):
        cols = pl.ds(pl.multiple_of(i * CHUNK, CHUNK), CHUNK)
        src_hot = onehot(src_ids[:, cols], ROWS)
        dst_hot = onehot(dst_ids[:, cols], ROWS)
        rel_hot = onehot(rel_ids[:, cols], NREL)
        s_re, s_im = both(jnp.dot(table2[...], src_hot, preferred_element_type=F32))
        d_re, d_im = both(jnp.dot(part2[...], dst_hot, preferred_element_type=F32))
        r_re, r_im = both(jnp.dot(rel2[...], rel_hot, preferred_element_type=F32))
        q_re, q_im = product(s_re, s_im, r_re, r_im)
        positive = jnp.sum(q_re * d_re + q_im * d_im, axis=0, keepdims=True)
        pos_coef = -jax.nn.sigmoid(-positive)
        query_b = jnp.concatenate([q_re, q_im], axis=0).astype(BF16)
        scores = jnp.dot(negs_t[...], query_b, preferred_element_type=F32)
        coef = (0.5 * weight + 0.5 * weight * jnp.tanh(0.5 * scores)).astype(BF16)
        neg_grad[:, :NNEG] += lax.dot_general(
            query_b, coef, BY_COLS, preferred_element_type=F32
        )
        g = jnp.dot(negs[...], coef, preferred_element_type=F32)
        g_re = pos_coef * d_re + g[:HALF]
        g_im = pos_coef * d_im + g[HALF:]
        put_split(spread, *back(g_re, g_im, r_re, r_im))
        src_acc[...] += lax.dot_general(spread[...], src_hot, BY_COLS, preferred_element_type=F32)
        put_split(spread, pos_coef * q_re, pos_coef * q_im)
        dst_acc[...] += lax.dot_general(spread[...], dst_hot, BY_COLS, preferred_element_type=F32)
        put_split(spread, *back(g_re, g_im, s_re, s_im))
        rel_acc[...] += lax.dot_general(spread[...], rel_hot, BY_COLS, preferred_element_type=F32)

    src_out[...] = src_acc[:DIM] + src_acc[DIM:]
    dst_out[...] = dst_acc[:DIM] + dst_acc[DIM:]
    rel_out[...] = (rel_acc[:DIM] + rel_acc[DIM:]).T

    for k in range(N_EDGE):
        first = ends[k] - quotas[0, k]
        parts = neg_grad[:, pl.ds(pl.multiple_of(first * BLOCK, BLOCK), QMAX * BLOCK)]
        hots = []
        for b in range(QMAX):
            hot = onehot(neg_ids[k * QMAX + b : k * QMAX + b + 1, :], ROWS)
            hots.append(jnp.where(b < quotas[0, k], hot, jnp.zeros_like(hot)))
        hot = jnp.concatenate(hots, axis=1)
        high, low_part = split(parts)
        summed = lax.dot_general(high, hot, BY_COLS, preferred_element_type=F32)
        summed += lax.dot_general(low_part, hot, BY_COLS, preferred_element_type=F32)
        dense_out[k] = summed


def step(quotas, table, shards, low, relation, src_ids, dst_ids, rel_ids, neg_ids):
    vmem = pl.BlockSpec(memory_space=VMEM)
    return pl.pallas_call(
        step_kernel,
        out_shape=(
            jax.ShapeDtypeStruct((N_EDGE, DIM, ROWS), F32),
            jax.ShapeDtypeStruct((DIM, ROWS), F32),
            jax.ShapeDtypeStruct((DIM, ROWS), F32),
            jax.ShapeDtypeStruct((NREL, DIM), F32),
        ),
        in_specs=[pl.BlockSpec(memory_space=SMEM)] + [vmem] * 8,
        out_specs=(vmem,) * 4,
        scratch_shapes=[
            VMEM((2 * DIM, ROWS), BF16),
            VMEM((2 * DIM, ROWS), BF16),
            VMEM((2 * DIM, NREL), BF16),
            VMEM((DIM, NNEG), BF16),
            VMEM((NNEG, DIM), BF16),
            VMEM((DIM, SLOT_COLS), F32),
            VMEM((2 * DIM, CHUNK), BF16),
            VMEM((2 * DIM, ROWS), F32),
            VMEM((2 * DIM, ROWS), F32),
            VMEM((2 * DIM, NREL), F32),
        ],
        compiler_params=pltpu.CompilerParams(vmem_limit_bytes=60 * 2**20),
        name="edges",
    )(quotas, table, shards, low, relation, src_ids, dst_ids, rel_ids, neg_ids)


def adagrad(table, state, grad):
    new_state = state + jnp.sum(grad * grad, axis=0, keepdims=True) * (1.0 / DIM)
    return table - learn_rate * grad / jnp.sqrt(new_state), new_state


def finish_kernel(
    dense, dst_grad, src_grad, rel_grad, src_table, src_state, part_high, part_low, part_state,
    relation, src_out, src_state_out, dst_out, dst_state_out, relation_out,
    give, taken, comb, sent_right, sent_left, got_right, got_left, rel_rows, rel_sums, rel_all,
    core_send, core_recv, right_send, right_recv, left_send, left_recv,
    rel_send, rel_recv,
):
    p = lax.axis_index("dom")
    e = lax.axis_index("edge")
    z, core = e // 2, e % 2
    right = ((z + 1) % N_Z) * 2 + core
    left = ((z + N_Z - 1) % N_Z) * 2 + core
    sibling = z * 2 + 1 - core
    dom_others = [(p + k) % N_DOM for k in range(1, N_DOM)]
    edge_others = [(e + k) % N_EDGE for k in range(1, N_EDGE)]
    order = [FAR]
    for d in range(FAR - 1, 0, -1):
        order += [d, N_Z - d]
    order.append(0)

    for d in order:
        give[d] = dense[((z + d) % N_Z) * 2 + 1 - core].astype(BF16)

    greet([(t, e) for t in dom_others] + [(p, t) for t in edge_others])

    core_copies = {}
    for d in order:
        copy = remote(give.at[d], taken.at[d], core_send.at[d], core_recv.at[d], p, sibling)
        copy.start()
        core_copies[d] = copy

    rel_copies = []
    first = []
    for k, t in enumerate(dom_others):
        copy = remote(
            rel_grad.at[t], rel_rows.at[p], rel_send.at[0, k], rel_recv.at[0, k], t, e
        )
        copy.start()
        first.append(copy)
    rel_rows[p] = rel_grad[p]

    ring = {}
    for d in order:
        core_copies[d].wait_recv()
        comb[d] = dense[((z + d) % N_Z) * 2 + core] + taken[d].astype(F32)

    copies = []
    for step in range(FAR):
        d = FAR - step
        for half in range(2):
            start, size = CUT[half]
            rows = pl.ds(start, size)
            for to_right in (True, False):
                if step == 0 and to_right != (half == 0):
                    continue
                place = d if to_right else (N_Z - d) % N_Z
                value = comb[place, rows]
                came = step >= 2 or (step == 1 and to_right == (half == 0))
                got = got_right if to_right else got_left
                sent = sent_right if to_right else sent_left
                if came:
                    ring[to_right, half].wait_recv()
                    value = value + got[step - 1, rows].astype(F32)
                sent[step, rows] = value.astype(BF16)
                send, recv = (right_send, right_recv) if to_right else (left_send, left_recv)
                copy = remote(
                    sent.at[step, rows], got.at[step, rows],
                    send.at[step, half], recv.at[step, half], p, right if to_right else left,
                )
                copy.start()
                ring[to_right, half] = copy
                copies.append(copy)

    for copy in first:
        copy.wait_recv()
    rel_sums[e] = jnp.sum(rel_rows[...], axis=0)
    second = []
    for k, t in enumerate(edge_others):
        copy = remote(
            rel_sums.at[e], rel_sums.at[e], rel_send.at[1, k], rel_recv.at[1, k], p, t
        )
        copy.start()
        second.append(copy)

    src_out[...], src_state_out[...] = adagrad(src_table[...], src_state[...], src_grad[...])

    for copy in second:
        copy.wait_recv()
    rel_all[p] = jnp.sum(rel_sums[...], axis=0)
    third = []
    for k, t in enumerate(dom_others):
        copy = remote(rel_all.at[p], rel_all.at[p], rel_send.at[2, k], rel_recv.at[2, k], t, e)
        copy.start()
        third.append(copy)

    for half in range(2):
        ring[True, half].wait_recv()
        ring[False, half].wait_recv()
    grad = dst_grad[...] + comb[0]
    grad = grad + got_right[FAR - 1].astype(F32) + got_left[FAR - 1].astype(F32)
    part = part_high[...].astype(F32) + part_low[...].astype(F32)
    dst_out[...], dst_state_out[...] = adagrad(part, part_state[...], grad)

    for copy in third:
        copy.wait_recv()
    relation_out[...] = relation[...] - rel_rate * rel_all[...]

    for copy in copies + first + second + third + list(core_copies.values()):
        copy.wait_send()


def finish(dense, dst_grad, src_grad, rel_grad, src_table, src_state, high, low, state, relation):
    dma = pltpu.SemaphoreType.DMA
    vmem = pl.BlockSpec(memory_space=VMEM)
    return pl.pallas_call(
        finish_kernel,
        out_shape=(
            jax.ShapeDtypeStruct((DIM, ROWS), F32),
            jax.ShapeDtypeStruct((1, ROWS), F32),
            jax.ShapeDtypeStruct((DIM, ROWS), F32),
            jax.ShapeDtypeStruct((1, ROWS), F32),
            jax.ShapeDtypeStruct((NREL, 1, DIM), F32),
        ),
        in_specs=[vmem] * 10,
        out_specs=(vmem,) * 5,
        scratch_shapes=[
            VMEM((N_Z, DIM, ROWS), BF16),
            VMEM((N_Z, DIM, ROWS), BF16),
            VMEM((N_Z, DIM, ROWS), F32),
            VMEM((FAR, DIM, ROWS), BF16),
            VMEM((FAR, DIM, ROWS), BF16),
            VMEM((FAR, DIM, ROWS), BF16),
            VMEM((FAR, DIM, ROWS), BF16),
            VMEM((N_DOM, 1, DIM), F32),
            VMEM((N_EDGE, 1, DIM), F32),
            VMEM((NREL, 1, DIM), F32),
            dma((N_Z,)), dma((N_Z,)),
            dma((FAR, 2)), dma((FAR, 2)), dma((FAR, 2)), dma((FAR, 2)),
            dma((3, N_DOM - 1)), dma((3, N_DOM - 1)),
        ],
        compiler_params=pltpu.CompilerParams(
            collective_id=1, has_side_effects=True, vmem_limit_bytes=60 * 2**20
        ),
        name="reduce_and_update",
    )(dense, dst_grad, src_grad, rel_grad, src_table, src_state, high, low, state, relation)


def shards(
    src_table,
    src_state,
    dst_table,
    dst_state,
    relation,
    edge_src,
    edge_dst,
    edge_rel,
    matching,
    neg_rows,
    quotas,
):
    gathered, low, state = pair(matching, dst_table, dst_state.reshape(1, ROWS))
    dense, dst_grad, src_grad, rel_grad = step(
        quotas,
        src_table,
        gathered,
        low,
        relation,
        edge_src.reshape(1, EDGES),
        edge_dst.reshape(1, EDGES),
        edge_rel.reshape(1, EDGES),
        neg_rows.reshape(N_EDGE * QMAX, BLOCK),
    )
    high = lax.dynamic_index_in_dim(gathered, lax.axis_index("edge"), 0, False)
    src_out, src_state_out, dst_out, dst_state_out, relation_out = finish(
        dense,
        dst_grad,
        src_grad,
        rel_grad.reshape(NREL, 1, DIM),
        src_table,
        src_state.reshape(1, ROWS),
        high,
        low,
        state,
        relation.T.reshape(NREL, 1, DIM),
    )
    return (
        src_out,
        src_state_out.reshape(ROWS),
        dst_out,
        dst_state_out.reshape(ROWS),
        relation_out.reshape(NREL, DIM).T,
    )


def solution(mesh):
    in_specs = (
        P(None, ("dom", "edge")),
        P(("dom", "edge")),
        P(None, ("dom", "edge")),
        P(("dom", "edge")),
        P(),
        P(("dom", "edge")),
        P(("dom", "edge")),
        P(("dom", "edge")),
        P(),
        P(("dom", "edge"), None, None),
        P(("dom", "edge"), None),
    )
    out_specs = (
        P(None, ("dom", "edge")),
        P(("dom", "edge")),
        P(None, ("dom", "edge")),
        P(("dom", "edge")),
        P(),
    )
    return jax.shard_map(shards, mesh=mesh, in_specs=in_specs, out_specs=out_specs, check_vma=False)
```

time: 794 us -> 206 us (0.26)
  local copies, waits for them, and re-layouts: 211 us -> 18.6 us
  Pallas kernels: 0 us -> 187 us
  waiting for transfers between devices: 178 us -> 0 us
  other arithmetic: 177 us -> 0 us
  blocking collectives: 98.4 us -> 0 us
  matrix products: 89.6 us -> 0 us
  starting transfers between devices: 18 us -> 0 us
  between operations: 14.9 us -> 0.67 us
    pallas_call x0 -> x3, Pallas kernels: none -> 187 us  [the longest x1 68.9 us: pair(): pl.pallas_call(pair_kernel, out_shape=(jax.ShapeDtypeStruct((N_EDGE, DIM,...]
    gather x36 -> x0, local copies, waits for them, and re-layouts: 116 us -> none  [the longest x16 50.8 us: edge_block(): src_rows = src_table[:, src_ids]]
    all_gather x1 -> x0, waiting for transfers between devices: 103 us -> none  [shards(): lax.all_gather(dst_table, 'dom', axis=1, tiled=True)]
    scatter-add x17 -> x0, other arithmetic: 91.5 us -> none  [the longest x8 37.2 us: edge_block(): src_grad = src_grad.at[:, src_ids].add(conj_product(query_grad, rel_edges))]
    dot_general x40 -> x0, matrix products: 89.6 us -> none  [the longest x8 36.6 us: edge_block(): jnp.dot(query_b, neg_coef, preferred_element_type=jnp.float32)]
    psum x1 -> x0, blocking collectives: 79.7 us -> none  [shards(): rel_total = lax.psum(rel_grad, ('dom', 'edge'))]
    all_to_all x2 -> x0, waiting for transfers between devices: 75.6 us -> none  [the longest x1 69.5 us: shards(): lax.all_to_all(served, 'edge', split_axis=1, concat_axis=1, tiled=True)]
    while x257 -> x0, local copies, waits for them, and re-layouts: 29 us -> none
  transfers between devices with their start and end apart: 4 -> 0, of which waited for: 3 -> 0; matrix products, arithmetic and copies ran while one was open for 1% -> 0% of each run, Pallas kernels for 0% -> 0%
where the time goes in v1:
time: 206 us
  Pallas kernels  187 us (91%)
  local copies, waits for them, and re-layouts  18.6 us (9%)
    pallas_call x1, Pallas kernels, pair(): pl.pallas_call(pair_kernel, out_shape=(jax.ShapeDtypeStruct((N_EDGE, DIM,...  68.9 us
    pallas_call x1, Pallas kernels, finish(): pl.pallas_call(finish_kernel, out_shape=(jax.ShapeDtypeStruct((DIM, ROWS)...  61.2 us
    pallas_call x1, Pallas kernels, step(): pl.pallas_call(step_kernel, out_shape=(jax.ShapeDtypeStruct((N_EDGE, DIM,...  56.4 us
    unnamed x18, local copies, waits for them, and re-layouts  13.4 us

profile of v1, /device:TPU:1, one launch (start us, length us, event | category | flops | bytes accessed | tf_op | source)
XLA Modules:
  0.0 205.8 jit_solution(17077879718875530341)
XLA Ops:
  0.6 0.0 copy-start.1
  0.6 1.1 copy-done.1
  1.8 0.0 copy-start.2
  1.8 0.7 copy-done.2
  2.5 0.0 copy-start.4
  2.5 0.7 copy-done.4
  3.1 0.0 copy-start.5
  3.1 68.9 %pair_and_gather.1 = (bf16[16,400,512]{2,1,0:T(8,128)(2,1)}, bf16[400,512]{1,0:T(8,128)(2,1)S(1)}, f32[1,512]{1,0:T(1,128)S(1)}) custom-call(s32[16]{0:T(128)S(1)} %copy-done.4, f32[400,512]{1,0:T(8,128)S(1)} %copy-done.1, f32[1,512]{1,0:T(1,128)S(1)} %bitcast.15), custom_call_target="tpu_custom_call" | custom-call | tf_op jit(solution)/shard_map/pair_and_gather/pallas_call | solution.py:203
  72.0 0.0 copy-start
  72.0 0.8 copy-done
  72.8 0.0 copy-start.3
  72.8 0.6 copy-done.3
  73.4 1.6 copy.16.relation
  74.9 1.3 reshape.47.neg_ids
  76.2 56.4 %edges.1 = (f32[16,400,512]{2,1,0:T(8,128)}, f32[400,512]{1,0:T(8,128)}, f32[400,512]{1,0:T(8,128)}, f32[16,400]{1,0:T(8,128)}) custom-call(s32[1,16]{1,0:T(1,128)} %quotas.1, f32[400,512]{1,0:T(8,128)} %src_table.1, bf16[16,400,512]{2,1,0:T(8,128)(2,1)} %get-tuple-element.17.shards, bf16[400,512]{1,0:T(8,128)(2,1)} %copy-done, f32[400,16]{1,0:T(8,128)} %copy.16.relation, ...), custom_call_target="tpu_custom_call" | custom-call | tf_op jit(solution)/shard_map/edges/pallas_call | solution.py:348
  132.7 1.4 reshape.48.rel_grad
  134.0 1.8 dynamic-slice_bitcast_fusion.part_high
  135.8 0.0 copy-done.5
  135.8 0.6 reshape.50.relation
  136.5 61.2 %reduce_and_update.1 = (f32[400,512]{1,0:T(8,128)}, f32[1,512]{1,0:T(1,128)}, f32[400,512]{1,0:T(8,128)}, f32[1,512]{1,0:T(1,128)}, f32[16,1,400]{2,1,0:T(1,128)}) custom-call(f32[16,400,512]{2,1,0:T(8,128)} %get-tuple-element.19.dense, f32[400,512]{1,0:T(8,128)} %get-tuple-element.20.dst_grad, f32[400,512]{1,0:T(8,128)} %get-tuple-element.21.src_grad, ...), custom_call_target="tpu_custom_call" | custom-call | tf_op jit(solution)/shard_map/reduce_and_update/pallas_call | solution.py:494
  197.7 1.4 copy.19
  199.1 2.1 %copy.24 = f32[400,512]{1,0:T(8,128)} copy(f32[400,512]{1,0:T(8,128)} %get-tuple-element.34) | data formatting | bytes 1638400
  201.2 1.3 copy.25
  202.4 2.1 %copy.26 = f32[400,512]{1,0:T(8,128)} copy(f32[400,512]{1,0:T(8,128)} %get-tuple-element.36) | data formatting | bytes 1638400
  204.5 1.2 copy.27
Async XLA Ops:
  0.6 1.1 copy-start.1
  1.8 0.7 copy-start.2
  2.5 0.7 copy-start.4
  3.1 132.7 %copy-start.5 = (f32[400,16]{0,1:T(8,128)S(1)}, f32[400,16]{0,1:T(8,128)}, u32[]{:S(2)}) copy-start(f32[400,16]{0,1:T(8,128)} %param.15) | copy-start | bytes 76804
  72.0 0.8 copy-start
  72.8 0.6 copy-start.3

commit v2 on v0

v2 whole, which is shorter than its diff:
```python
import math

import jax
import jax.numpy as jnp
from jax import lax
from jax.experimental import pallas as pl
from jax.experimental.pallas import tpu as pltpu
from jax.sharding import PartitionSpec as P

DIM = 400
HALF = 200
NREL = 16
BLOCK = 128
QMAX = 2
QTOTAL = 12
NNEG = 1536
ROWS = 512
EDGES = 4096
N_DOM = 16
N_EDGE = 16
N_Z = 8
FAR = N_Z // 2
DISTANCES = (4, 3, 5, 2, 6, 1, 7, 0)
NEAR_FROM = 512

PIECE_ROWS = 112
PIECE_COLS = 128
PAD_DIM = 448
CUT = ((0, 208), (208, 192))

CHUNK = 512
N_CHUNK = EDGES // CHUNK

learn_rate = 0.1
rel_rate = 0.02
weight = 1.0 / math.sqrt(NNEG)

F32 = jnp.float32
BF16 = jnp.bfloat16
VMEM = pltpu.VMEM
HBM = pl.ANY
SMEM = pltpu.SMEM
BY_COLS = (((1,), (1,)), ((), ()))


def on(p, e):
    return {"dom": p, "edge": e}


def remote(src, dst, send_sem, recv_sem, p, e):
    return pltpu.make_async_remote_copy(
        src_ref=src,
        dst_ref=dst,
        send_sem=send_sem,
        recv_sem=recv_sem,
        device_id=on(p, e),
        device_id_type=pl.DeviceIdType.MESH,
    )


def greet(devices):
    barrier = pltpu.get_barrier_semaphore()
    for p, e in devices:
        pl.semaphore_signal(
            barrier, inc=1, device_id=on(p, e), device_id_type=pl.DeviceIdType.MESH
        )
    pl.semaphore_wait(barrier, len(devices))


def split(x):
    high = x.astype(BF16)
    return high, (x - high.astype(F32)).astype(BF16)


def piece(k):
    rows = pl.ds(pl.multiple_of((k // 4) * PIECE_ROWS, 16), PIECE_ROWS)
    cols = pl.ds(pl.multiple_of((k % 4) * PIECE_COLS, 128), PIECE_COLS)
    return rows, cols


def product(x_re, x_im, y_re, y_im):
    return x_re * y_re - x_im * y_im, x_re * y_im + x_im * y_re


def back(g_re, g_im, v_re, v_im):
    return g_re * v_re + g_im * v_im, g_im * v_re - g_re * v_im


def onehot(ids, count):
    places = lax.broadcasted_iota(jnp.int32, (count, ids.shape[1]), 0)
    return jnp.where(places == ids, 1.0, 0.0).astype(BF16)


def put_split(ref, re, im):
    x = jnp.concatenate([re, im], axis=0)
    high, low = split(x)
    ref[:DIM] = high
    ref[DIM:] = low


def both(x):
    return x[:HALF] + x[DIM : DIM + HALF], x[HALF:DIM] + x[DIM + HALF :]


def plan_kernel(quotas, neg_rows, plan, slots):
    e = lax.axis_index("edge")
    z, core = e // 2, e % 2
    owners, ends = [], []
    total = 0
    for g in range(N_EDGE):
        owner = ((z + DISTANCES[g // 2]) % N_Z) * 2 + (core if g % 2 == 0 else 1 - core)
        plan[2 * QTOTAL + g] = total
        total = total + quotas[0, owner]
        owners.append(owner)
        ends.append(total)
    for j in range(QTOTAL):
        owner = owners[0]
        first = 0
        for g in range(1, N_EDGE):
            owner = jnp.where(ends[g - 1] <= j, owners[g], owner)
            first = jnp.where(ends[g - 1] <= j, ends[g - 1], first)
        plan[j] = owner
        plan[QTOTAL + j] = owner * QMAX + jnp.clip(j - first, 0, QMAX - 1)
    lanes = lax.broadcasted_iota(jnp.int32, (1, QMAX * BLOCK), 1)
    for k in range(N_EDGE):
        live = jnp.where(lanes < quotas[0, k] * BLOCK, neg_rows[k : k + 1], -1)
        for b in range(QMAX):
            slots[k * QMAX + b] = live[:, b * BLOCK : (b + 1) * BLOCK]


def make_plan(quotas, neg_rows):
    smem = pl.BlockSpec(memory_space=SMEM)
    vmem = pl.BlockSpec(memory_space=VMEM)
    return pl.pallas_call(
        plan_kernel,
        out_shape=(
            jax.ShapeDtypeStruct((2 * QTOTAL + N_EDGE,), jnp.int32),
            jax.ShapeDtypeStruct((N_EDGE * QMAX, 1, BLOCK), jnp.int32),
        ),
        in_specs=[smem, vmem],
        out_specs=(smem, vmem),
        name="plan",
    )(quotas, neg_rows)


def kernel(
    matching, plan, table, state, src_table_hbm, src_state, relation,
    src_ids, dst_ids, rel_ids, slots,
    src_step_out, src_state_out, part_out, dst_step_out, dst_state_out, rel_out,
    shards, low, own, landed_high, landed_low, picked, states, src_table,
    table2, part2, rel2, query_b, hold, coefs, negs, negs_t, neg_grad, spread,
    src_acc, dst_acc, rel_acc, taken, got_right, got_left,
    rel_mine, rel_rows, rel_sums,
    own_send, own_recv, pick_send, pick_recv, state_send, state_recv,
    right_send, right_recv, left_send, left_recv, core_send, core_recv,
    give_send, give_recv, down_send, down_recv, up_send, up_recv,
    rel_send, rel_recv, local_sem,
):
    p = lax.axis_index("dom")
    e = lax.axis_index("edge")
    z, core = e // 2, e % 2
    right = ((z + 1) % N_Z) * 2 + core
    left = ((z + N_Z - 1) % N_Z) * 2 + core
    sibling = z * 2 + 1 - core
    others = [(p + k) % N_DOM for k in range(1, N_DOM)]
    edge_others = [(e + k) % N_EDGE for k in range(1, N_EDGE)]
    rows_p, cols_p = piece(p)
    sent = []

    fetch = pltpu.make_async_copy(src_table_hbm, src_table, local_sem.at[0])
    fetch.start()
    own[0, :DIM], own[1, :DIM] = split(table[...])
    own[:, DIM:] = jnp.zeros((2, PAD_DIM - DIM, ROWS), BF16)
    states[p] = state[...]

    greet([(t, e) for t in others] + [(p, t) for t in edge_others])

    landed = (landed_high, landed_low)

    def spread_pieces(part):
        copies = []
        for k, t in enumerate(others):
            rows, cols = piece(t)
            copy = remote(
                own.at[part, rows, cols], landed[part].at[p],
                own_send.at[part, k], own_recv.at[part, k], t, e,
            )
            copy.start()
            copies.append(copy)
        landed[part][p] = own[part, rows_p, cols_p]
        sent.extend(copies)
        return copies

    def pick(part, came, target_ref):
        for copy in came:
            copy.wait_recv()
        copies = []
        for k, t in enumerate(others):
            picked[part, k] = landed[part][matching[t]]
            copy = remote(
                picked.at[part, k], target_ref.at[rows_p, cols_p],
                pick_send.at[part, k], pick_recv.at[part, k], t, e,
            )
            copy.start()
            copies.append(copy)
        target_ref[rows_p, cols_p] = landed[part][matching[p]]
        sent.extend(copies)
        return copies

    came_high = spread_pieces(0)

    rel_acc[...] = jnp.zeros_like(rel_acc)
    src_acc[...] = jnp.zeros_like(src_acc)
    dst_acc[...] = jnp.zeros_like(dst_acc)
    neg_grad[...] = jnp.zeros_like(neg_grad)
    rel2[:DIM], rel2[DIM:] = split(relation[...].T)
    fetch.wait()
    table2[:DIM], table2[DIM:] = split(src_table[...])

    def chunk_cols(i):
        return pl.ds(pl.multiple_of(i * CHUNK, CHUNK), CHUNK)

    def source_rows(cols):
        src_hot = onehot(src_ids[:, cols], ROWS)
        rel_hot = onehot(rel_ids[:, cols], NREL)
        s_re, s_im = both(jnp.dot(table2[...], src_hot, preferred_element_type=F32))
        r_re, r_im = both(jnp.dot(rel2[...], rel_hot, preferred_element_type=F32))
        return src_hot, rel_hot, s_re, s_im, r_re, r_im

    def queries(first, last):
        @pl.loop(first, last)
        def _(i):
            cols = chunk_cols(i)
            _, _, s_re, s_im, r_re, r_im = source_rows(cols)
            q_re, q_im = product(s_re, s_im, r_re, r_im)
            hold[:HALF, cols] = q_re
            hold[HALF:, cols] = q_im
            query_b[:, cols] = jnp.concatenate([q_re, q_im], axis=0).astype(BF16)

    def positives(first, last):
        @pl.loop(first, last)
        def _(i):
            cols = chunk_cols(i)
            dst_hot = onehot(dst_ids[:, cols], ROWS)
            d_re, d_im = both(jnp.dot(part2[...], dst_hot, preferred_element_type=F32))
            q_re, q_im = hold[:HALF, cols], hold[HALF:, cols]
            positive = jnp.sum(q_re * d_re + q_im * d_im, axis=0, keepdims=True)
            pos_coef = -jax.nn.sigmoid(-positive)
            put_split(spread, pos_coef * q_re, pos_coef * q_im)
            dst_acc[...] += lax.dot_general(
                spread[...], dst_hot, BY_COLS, preferred_element_type=F32
            )
            hold[:HALF, cols] = pos_coef * d_re
            hold[HALF:, cols] = pos_coef * d_im

    came_high = pick(0, came_high, shards.at[e])
    queries(0, 2)
    for copy in came_high:
        copy.wait_recv()

    flying = {}

    def go(step, half, to_right):
        source = ((z - step + N_Z) % N_Z if to_right else (z + step) % N_Z) * 2 + core
        start, size = CUT[half]
        ref = shards.at[source, pl.ds(start, size)]
        sems = (right_send, right_recv) if to_right else (left_send, left_recv)
        copy = remote(
            ref, ref, sems[0].at[step, half], sems[1].at[step, half],
            p, right if to_right else left,
        )
        copy.start()
        sent.append(copy)
        flying[to_right, half] = copy

    across = []

    def cross(slot, source_z, half):
        start, size = CUT[half]
        ref = shards.at[source_z * 2 + core, pl.ds(start, size)]
        copy = remote(ref, ref, core_send.at[slot, half], core_recv.at[slot, half], p, sibling)
        copy.start()
        across.append(copy)

    def forward(step, half):
        for to_right in (True, False):
            if step == FAR and to_right != (half == 0):
                continue
            flying[to_right, half].wait_recv()
            source_z = (z - step + N_Z) % N_Z if to_right else (z + step) % N_Z
            if step < FAR - 1 or (step == FAR - 1 and to_right == (half == 0)):
                go(step, half, to_right)
            if step == FAR:
                slot = 2 * FAR - 1
            else:
                slot = 2 * step - 1 if to_right else 2 * step
            cross(slot, source_z, half)

    for half in range(2):
        go(0, half, True)
        go(0, half, False)
    for half in range(2):
        cross(0, z, half)
    came_low = spread_pieces(1)
    state_copies = []
    for k, t in enumerate(others):
        copy = remote(states.at[p], states.at[p], state_send.at[k], state_recv.at[k], t, e)
        copy.start()
        state_copies.append(copy)
    sent.extend(state_copies)

    queries(2, 5)
    came_low = pick(1, came_low, low)
    forward(1, 0)
    queries(5, 8)
    forward(1, 1)
    part2[:DIM] = shards[e, :DIM]
    for copy in came_low:
        copy.wait_recv()
    part2[DIM:] = low[:DIM]
    part_done = pltpu.make_async_copy(part2, part_out, local_sem.at[1])
    part_done.start()
    positives(0, 2)
    forward(2, 0)
    positives(2, 4)
    forward(2, 1)
    positives(4, 6)
    forward(3, 0)
    positives(6, 7)
    forward(3, 1)
    positives(7, 8)
    forward(4, 0)
    forward(4, 1)
    for copy in across:
        copy.wait()

    for j in range(QTOTAL):
        hot = onehot(slots[plan[QTOTAL + j]], ROWS)
        found = jnp.dot(shards[plan[j], :DIM], hot, preferred_element_type=F32)
        negs[:, j * BLOCK : (j + 1) * BLOCK] = found.astype(BF16)
        negs_t[j * BLOCK : (j + 1) * BLOCK, :] = found.T.astype(BF16)

    def negatives(first, last):
        @pl.loop(0, N_CHUNK)
        def _(i):
            cols = chunk_cols(i)
            scores = jnp.dot(
                negs_t[first:last], query_b[:, cols], preferred_element_type=F32
            )
            coef = (0.5 * weight + 0.5 * weight * jnp.tanh(0.5 * scores)).astype(BF16)
            coefs[first:last, cols] = coef
            added = lax.dot_general(
                query_b[:, cols], coef, BY_COLS, preferred_element_type=F32
            )
            for j in range(first // BLOCK, last // BLOCK):
                at = j * BLOCK - first
                neg_grad[j] += added[:, at : at + BLOCK]

    for copy in sent:
        copy.wait_send()
    sent.clear()

    give_copies = {}

    def dense(g):
        first = plan[2 * QTOTAL + g]
        owner = ((z + DISTANCES[g // 2]) % N_Z) * 2 + (core if g % 2 == 0 else 1 - core)
        parts = jnp.concatenate([neg_grad[first + b] for b in range(QMAX)], axis=1)
        ids = jnp.concatenate([slots[owner * QMAX + b] for b in range(QMAX)], axis=1)
        hot = onehot(ids, ROWS)
        high, low_part = split(parts)
        summed = lax.dot_general(high, hot, BY_COLS, preferred_element_type=F32)
        return summed + lax.dot_general(low_part, hot, BY_COLS, preferred_element_type=F32)

    def contribute(at):
        d = DISTANCES[at]
        shards[N_Z + d, :DIM] = dense(2 * at + 1).astype(BF16)
        copy = remote(
            shards.at[N_Z + d, pl.ds(0, DIM)], taken.at[d],
            give_send.at[d], give_recv.at[d], p, sibling,
        )
        copy.start()
        sent.append(copy)
        give_copies[d] = copy
        shards[d, :DIM] = dense(2 * at).astype(BF16)

    joined = set()
    ring = {}

    def reduce_step(step, half):
        d = FAR - step
        start, size = CUT[half]
        rows = pl.ds(start, size)
        for to_right in (True, False):
            if step == 0 and to_right != (half == 0):
                continue
            place = d if to_right else (N_Z - d) % N_Z
            if place not in joined:
                give_copies[place].wait_recv()
                joined.add(place)
            value = shards[place, rows].astype(F32) + taken[place, rows].astype(F32)
            got = got_right if to_right else got_left
            if step >= 2 or (step == 1 and to_right == (half == 0)):
                ring[to_right, half].wait_recv()
                value = value + got[step - 1, rows].astype(F32)
            shards[place, rows] = value.astype(BF16)
            send, recv = (down_send, down_recv) if to_right else (up_send, up_recv)
            copy = remote(
                shards.at[place, rows], got.at[step, rows],
                send.at[step, half], recv.at[step, half], p, right if to_right else left,
            )
            copy.start()
            ring[to_right, half] = copy
            sent.append(copy)

    def query_grads(first, last):
        @pl.loop(first, last)
        def _(i):
            cols = chunk_cols(i)
            src_hot, rel_hot, s_re, s_im, r_re, r_im = source_rows(cols)
            g = jnp.dot(negs[...], coefs[:, cols], preferred_element_type=F32)
            g_re = hold[:HALF, cols] + g[:HALF]
            g_im = hold[HALF:, cols] + g[HALF:]
            put_split(spread, *back(g_re, g_im, r_re, r_im))
            src_acc[...] += lax.dot_general(
                spread[...], src_hot, BY_COLS, preferred_element_type=F32
            )
            put_split(spread, *back(g_re, g_im, s_re, s_im))
            rel_acc[...] += lax.dot_general(
                spread[...], rel_hot, BY_COLS, preferred_element_type=F32
            )

    negatives(0, NEAR_FROM)
    contribute(0)
    reduce_step(0, 0)
    reduce_step(0, 1)
    negatives(NEAR_FROM, NNEG)
    contribute(1)
    contribute(2)
    reduce_step(1, 0)
    reduce_step(1, 1)
    contribute(3)
    contribute(4)
    query_grads(0, 2)
    reduce_step(2, 0)
    query_grads(2, 3)
    contribute(5)
    contribute(6)
    reduce_step(2, 1)
    query_grads(3, 5)
    contribute(7)
    reduce_step(3, 0)
    query_grads(5, 7)
    reduce_step(3, 1)
    query_grads(7, 8)

    rel_grad = (rel_acc[:DIM] + rel_acc[DIM:]).T
    for r in range(NREL):
        rel_mine[r] = rel_grad[r : r + 1]
    first_copies = []
    for k, t in enumerate(others):
        copy = remote(
            rel_mine.at[t], rel_rows.at[p], rel_send.at[0, k], rel_recv.at[0, k], t, e
        )
        copy.start()
        first_copies.append(copy)
    rel_rows[p] = rel_mine[p]

    new_state = src_state[...]
    grad = src_acc[:DIM] + src_acc[DIM:]
    src_step, src_state_out[...] = adagrad(new_state, grad)
    src_acc[:DIM] = src_step
    src_done = pltpu.make_async_copy(src_acc.at[pl.ds(0, DIM)], src_step_out, local_sem.at[2])
    src_done.start()

    for copy in first_copies:
        copy.wait_recv()
    rel_sums[e] = jnp.sum(rel_rows[...], axis=0)
    second_copies = []
    for k, t in enumerate(edge_others):
        copy = remote(
            rel_sums.at[e], rel_sums.at[e], rel_send.at[1, k], rel_recv.at[1, k], p, t
        )
        copy.start()
        second_copies.append(copy)

    dst_acc[:DIM] = dst_acc[:DIM] + dst_acc[DIM:]
    for copy in state_copies:
        copy.wait_recv()
    part_state = states[matching[p]]
    give_copies[0].wait_recv()
    dst_acc[:DIM] = dst_acc[:DIM] + shards[0, :DIM].astype(F32) + taken[0].astype(F32)

    for copy in second_copies:
        copy.wait_recv()
    rel_out[p] = jnp.sum(rel_sums[...], axis=0)
    third_copies = []
    for k, t in enumerate(others):
        copy = remote(rel_out.at[p], rel_out.at[p], rel_send.at[2, k], rel_recv.at[2, k], t, e)
        copy.start()
        third_copies.append(copy)

    for half in range(2):
        ring[True, half].wait_recv()
        ring[False, half].wait_recv()
    grad = dst_acc[:DIM] + got_right[FAR - 1].astype(F32) + got_left[FAR - 1].astype(F32)
    dst_step, dst_state_out[...] = adagrad(part_state, grad)
    dst_acc[:DIM] = dst_step
    dst_done = pltpu.make_async_copy(dst_acc.at[pl.ds(0, DIM)], dst_step_out, local_sem.at[3])
    dst_done.start()

    for copy in third_copies:
        copy.wait_recv()
    for copy in sent + first_copies + second_copies + third_copies:
        copy.wait_send()
    part_done.wait()
    src_done.wait()
    dst_done.wait()


def adagrad(state, grad):
    new_state = state + jnp.sum(grad * grad, axis=0, keepdims=True) * (1.0 / DIM)
    return learn_rate * grad / jnp.sqrt(new_state), new_state


def run(*args):
    dma = pltpu.SemaphoreType.DMA
    vmem = pl.BlockSpec(memory_space=VMEM)
    smem = pl.BlockSpec(memory_space=SMEM)
    hbm = pl.BlockSpec(memory_space=HBM)
    return pl.pallas_call(
        kernel,
        out_shape=(
            jax.ShapeDtypeStruct((DIM, ROWS), F32),
            jax.ShapeDtypeStruct((1, ROWS), F32),
            jax.ShapeDtypeStruct((2 * DIM, ROWS), BF16),
            jax.ShapeDtypeStruct((DIM, ROWS), F32),
            jax.ShapeDtypeStruct((1, ROWS), F32),
            jax.ShapeDtypeStruct((NREL, 1, DIM), F32),
        ),
        in_specs=[smem, smem, vmem, vmem, hbm] + [vmem] * 6,
        out_specs=(hbm, vmem, hbm, hbm, vmem, vmem),
        scratch_shapes=[
            VMEM((N_EDGE, PAD_DIM, ROWS), BF16),
            VMEM((PAD_DIM, ROWS), BF16),
            VMEM((2, PAD_DIM, ROWS), BF16),
            VMEM((N_DOM, PIECE_ROWS, PIECE_COLS), BF16),
            VMEM((N_DOM, PIECE_ROWS, PIECE_COLS), BF16),
            VMEM((2, N_DOM - 1, PIECE_ROWS, PIECE_COLS), BF16),
            VMEM((N_DOM, 1, ROWS), F32),
            VMEM((DIM, ROWS), F32),
            VMEM((2 * DIM, ROWS), BF16),
            VMEM((2 * DIM, ROWS), BF16),
            VMEM((2 * DIM, NREL), BF16),
            VMEM((DIM, EDGES), BF16),
            VMEM((DIM, EDGES), F32),
            VMEM((NNEG, EDGES), BF16),
            VMEM((DIM, NNEG), BF16),
            VMEM((NNEG, DIM), BF16),
            VMEM((QTOTAL + QMAX, DIM, BLOCK), F32),
            VMEM((2 * DIM, CHUNK), BF16),
            VMEM((2 * DIM, ROWS), F32),
            VMEM((2 * DIM, ROWS), F32),
            VMEM((2 * DIM, NREL), F32),
            VMEM((N_Z, DIM, ROWS), BF16),
            VMEM((FAR, DIM, ROWS), BF16),
            VMEM((FAR, DIM, ROWS), BF16),
            VMEM((NREL, 1, DIM), F32),
            VMEM((N_DOM, 1, DIM), F32),
            VMEM((N_EDGE, 1, DIM), F32),
            dma((2, N_DOM - 1)), dma((2, N_DOM - 1)),
            dma((2, N_DOM - 1)), dma((2, N_DOM - 1)),
            dma((N_DOM - 1,)), dma((N_DOM - 1,)),
            dma((FAR, 2)), dma((FAR, 2)), dma((FAR, 2)), dma((FAR, 2)),
            dma((N_Z, 2)), dma((N_Z, 2)),
            dma((N_Z,)), dma((N_Z,)),
            dma((FAR, 2)), dma((FAR, 2)), dma((FAR, 2)), dma((FAR, 2)),
            dma((3, N_DOM - 1)), dma((3, N_DOM - 1)),
            dma((4,)),
        ],
        compiler_params=pltpu.CompilerParams(
            collective_id=0, has_side_effects=True, vmem_limit_bytes=60 * 2**20
        ),
        name="bucket_step",
    )(*args)


def shards(
    src_table,
    src_state,
    dst_table,
    dst_state,
    relation,
    edge_src,
    edge_dst,
    edge_rel,
    matching,
    neg_rows,
    quotas,
):
    plan, slots = make_plan(quotas, neg_rows.reshape(N_EDGE, QMAX * BLOCK))
    src_step, src_state_out, part, dst_step, dst_state_out, rel_total = run(
        matching,
        plan,
        dst_table,
        dst_state.reshape(1, ROWS),
        src_table,
        src_state.reshape(1, ROWS),
        relation.T,
        edge_src.reshape(1, EDGES),
        edge_dst.reshape(1, EDGES),
        edge_rel.reshape(1, EDGES),
        slots,
    )
    return (
        src_table - src_step,
        src_state_out.reshape(ROWS),
        part[:DIM].astype(F32) + part[DIM:].astype(F32) - dst_step,
        dst_state_out.reshape(ROWS),
        relation - rel_rate * rel_total.reshape(NREL, DIM).T,
    )


def solution(mesh):
    in_specs = (
        P(None, ("dom", "edge")),
        P(("dom", "edge")),
        P(None, ("dom", "edge")),
        P(("dom", "edge")),
        P(),
        P(("dom", "edge")),
        P(("dom", "edge")),
        P(("dom", "edge")),
        P(),
        P(("dom", "edge"), None, None),
        P(("dom", "edge"), None),
    )
    out_specs = (
        P(None, ("dom", "edge")),
        P(("dom", "edge")),
        P(None, ("dom", "edge")),
        P(("dom", "edge")),
        P(),
    )
    return jax.shard_map(shards, mesh=mesh, in_specs=in_specs, out_specs=out_specs, check_vma=False)
```

time: 794 us -> 138 us (0.17)
  local copies, waits for them, and re-layouts: 211 us -> 2 us
  waiting for transfers between devices: 178 us -> 0 us
  other arithmetic: 177 us -> 4.01 us
  Pallas kernels: 0 us -> 131 us
  blocking collectives: 98.4 us -> 0 us
  matrix products: 89.6 us -> 0 us
  starting transfers between devices: 18 us -> 0 us
  between operations: 14.9 us -> 0.7 us
    pallas_call x0 -> x2, Pallas kernels: none -> 131 us  [the longest x1 129 us: run(): pl.pallas_call(kernel, out_shape=(jax.ShapeDtypeStruct((DIM, ROWS), F32),...]
    gather x36 -> x0, local copies, waits for them, and re-layouts: 116 us -> none  [the longest x16 50.8 us: edge_block(): src_rows = src_table[:, src_ids]]
    all_gather x1 -> x0, waiting for transfers between devices: 103 us -> none  [shards(): lax.all_gather(dst_table, 'dom', axis=1, tiled=True)]
    scatter-add x17 -> x0, other arithmetic: 91.5 us -> none  [the longest x8 37.2 us: edge_block(): src_grad = src_grad.at[:, src_ids].add(conj_product(query_grad, rel_edges))]
    dot_general x40 -> x0, matrix products: 89.6 us -> none  [the longest x8 36.6 us: edge_block(): jnp.dot(query_b, neg_coef, preferred_element_type=jnp.float32)]
    psum x1 -> x0, blocking collectives: 79.7 us -> none  [shards(): rel_total = lax.psum(rel_grad, ('dom', 'edge'))]
    all_to_all x2 -> x0, waiting for transfers between devices: 75.6 us -> none  [the longest x1 69.5 us: shards(): lax.all_to_all(served, 'edge', split_axis=1, concat_axis=1, tiled=True)]
    while x257 -> x0, local copies, waits for them, and re-layouts: 29 us -> none
  transfers between devices with their start and end apart: 4 -> 0, of which waited for: 3 -> 0; matrix products, arithmetic and copies ran while one was open for 1% -> 0% of each run, Pallas kernels for 0% -> 0%
where the time goes in v2:
time: 138 us; the launch traced here: 137 us
  Pallas kernels  131 us (95%)
  other arithmetic  4.01 us (3%)
  local copies, waits for them, and re-layouts  2 us (1%)
    pallas_call x1, Pallas kernels, run(): pl.pallas_call(kernel, out_shape=(jax.ShapeDtypeStruct((DIM, ROWS), F32),...  129 us

profile of v2, /device:TPU:1, one launch (start us, length us, event | category | flops | bytes accessed | tf_op | source)
XLA Modules:
  0.0 137.4 jit_solution(1315527940634412048)
XLA Ops:
  0.6 1.7 %plan.1 = (s32[40]{0:T(128)}, s32[32,1,128]{2,1,0:T(1,128)}) custom-call(s32[1,16]{1,0:T(1,128)} %quotas.1, s32[16,256]{1,0:T(8,128)} %bitcast.17), custom_call_target="tpu_custom_call" | custom-call | tf_op jit(solution)/shard_map/plan/pallas_call | solution.py:134
  2.4 0.0 copy-start
  2.4 128.9 %bucket_step.1 = (f32[400,512]{1,0:T(8,128)}, f32[1,512]{1,0:T(1,128)}, bf16[800,512]{1,0:T(8,128)(2,1)}, f32[400,512]{1,0:T(8,128)}, f32[1,512]{1,0:T(1,128)}, /*index=5*/f32[16,1,400]{2,1,0:T(1,128)}) custom-call(s32[16]{0:T(128)} %matching.1, s32[40]{0:T(128)} %get-tuple-element.13.plan, f32[400,512]{1,0:T(8,128)} %table.1, f32[1,512]{1,0:T(1,128)} %bitcast.18, ...), custom_call_target="tpu_custom_call" | custom-call | tf_op jit(solution)/shard_map/bucket_step/pallas_call | solution.py:531
  131.3 0.0 copy-done
  131.3 0.0 copy-start.4
  131.4 0.0 copy-start.1
  131.4 0.0 copy-start.2
  131.4 2.3 %sub.9 = f32[400,512]{1,0:T(8,128)} subtract(f32[400,512]{1,0:T(8,128)S(1)} %copy-done, f32[400,512]{1,0:T(8,128)} %get-tuple-element.15) | non-fusion elementwise | flops 204800 | bytes 2457600 | tf_op jit(solution)/shard_map/sub | solution.py:616
  133.7 0.0 copy-done.4
  133.7 0.0 copy-start.3
  133.7 0.7 copy-done.3
  134.4 0.6 bitcast_subtract_fusion
  135.1 0.0 copy-done.1
  135.1 0.0 copy-done.2
  135.1 0.0 copy-start.6
  135.1 1.1 add_subtract_fusion
  136.1 0.0 copy-done.6
  136.1 0.0 copy-start.5
  136.1 0.6 copy.20
  136.7 0.1 copy-done.5
  136.8 0.6 copy.21
  (1 shorter events, 0.0 us)
Async XLA Ops:
  2.4 128.9 %copy-start = (f32[400,512]{1,0:T(8,128)S(1)}, f32[400,512]{1,0:T(8,128)}, u32[]{:S(2)}) copy-start(f32[400,512]{1,0:T(8,128)} %src_table_hbm.1) | copy-start | bytes 2457604
  131.3 2.3 %copy-start.4 = (f32[16,1,400]{2,1,0:T(1,128)S(1)}, f32[16,1,400]{2,1,0:T(1,128)}, u32[]{:S(2)}) copy-start(f32[16,1,400]{2,1,0:T(1,128)} %get-tuple-element.20) | copy-start | bytes 76804
  131.4 3.7 %copy-start.1 = (bf16[800,512]{1,0:T(8,128)(2,1)S(1)}, bf16[800,512]{1,0:T(8,128)(2,1)}, u32[]{:S(2)}) copy-start(bf16[800,512]{1,0:T(8,128)(2,1)} %get-tuple-element.17) | copy-start | bytes 2457604
  131.4 3.7 %copy-start.2 = (f32[400,512]{1,0:T(8,128)S(1)}, f32[400,512]{1,0:T(8,128)}, u32[]{:S(2)}) copy-start(f32[400,512]{1,0:T(8,128)} %get-tuple-element.18) | copy-start | bytes 2457604
  133.7 0.8 copy-start.3
  135.1 1.1 copy-start.6
  136.1 0.7 copy-start.5

commit v3 on v2

--- a/solution.py
+++ b/solution.py
@@ -20,13 +20,13 @@
 N_EDGE = 16
 N_Z = 8
 FAR = N_Z // 2
-DISTANCES = (4, 3, 5, 2, 6, 1, 7, 0)
-NEAR_FROM = 512
-
-PIECE_ROWS = 112
+DISTANCES = (0, 7, 1, 6, 2, 5, 3, 4)
+NEAR_BLOCKS = 8
+
+PAIRED = ((0, 0, 48), (0, 192, 64), (1, 0, 112))
 PIECE_COLS = 128
 PAD_DIM = 448
-CUT = ((0, 208), (208, 192))
+CUT = ((0, 192), (192, 208))
 
 CHUNK = 512
 N_CHUNK = EDGES // CHUNK
@@ -72,8 +72,9 @@
     return high, (x - high.astype(F32)).astype(BF16)
 
 
-def piece(k):
-    rows = pl.ds(pl.multiple_of((k // 4) * PIECE_ROWS, 16), PIECE_ROWS)
+def piece(k, part):
+    _, start, size = PAIRED[part]
+    rows = pl.ds(pl.multiple_of(start + (k // 4) * size, 16), size)
     cols = pl.ds(pl.multiple_of((k % 4) * PIECE_COLS, 128), PIECE_COLS)
     return rows, cols
 
@@ -102,9 +103,14 @@
     return x[:HALF] + x[DIM : DIM + HALF], x[HALF:DIM] + x[DIM + HALF :]
 
 
-def plan_kernel(quotas, neg_rows, plan, slots):
+def plan_kernel(quotas, neg_rows, plan, slots, near_ids, far_ids):
     e = lax.axis_index("edge")
     z, core = e // 2, e % 2
+    lanes = lax.broadcasted_iota(jnp.int32, (1, QMAX * BLOCK), 1)
+    for k in range(N_EDGE):
+        live = jnp.where(lanes < quotas[0, k] * BLOCK, neg_rows[k : k + 1], -1)
+        for b in range(QMAX):
+            slots[k * QMAX + b] = live[:, b * BLOCK : (b + 1) * BLOCK]
     owners, ends = [], []
     total = 0
     for g in range(N_EDGE):
@@ -113,19 +119,19 @@
         total = total + quotas[0, owner]
         owners.append(owner)
         ends.append(total)
+    nearer = ends[N_EDGE - QMAX - 1]
     for j in range(QTOTAL):
         owner = owners[0]
         first = 0
         for g in range(1, N_EDGE):
             owner = jnp.where(ends[g - 1] <= j, owners[g], owner)
             first = jnp.where(ends[g - 1] <= j, ends[g - 1], first)
-        plan[j] = owner
-        plan[QTOTAL + j] = owner * QMAX + jnp.clip(j - first, 0, QMAX - 1)
-    lanes = lax.broadcasted_iota(jnp.int32, (1, QMAX * BLOCK), 1)
-    for k in range(N_EDGE):
-        live = jnp.where(lanes < quotas[0, k] * BLOCK, neg_rows[k : k + 1], -1)
-        for b in range(QMAX):
-            slots[k * QMAX + b] = live[:, b * BLOCK : (b + 1) * BLOCK]
+        rows = slots[owner * QMAX + jnp.clip(j - first, 0, QMAX - 1)]
+        plan[j] = jnp.where(j < nearer, owner, e)
+        plan[QTOTAL + j] = jnp.where(j < nearer, 0, owner % 2)
+        near_ids[j] = jnp.where(j < nearer, rows, -1)
+        if j >= NEAR_BLOCKS:
+            far_ids[j - NEAR_BLOCKS] = jnp.where(j < nearer, -1, rows)
 
 
 def make_plan(quotas, neg_rows):
@@ -136,18 +142,21 @@
         out_shape=(
             jax.ShapeDtypeStruct((2 * QTOTAL + N_EDGE,), jnp.int32),
             jax.ShapeDtypeStruct((N_EDGE * QMAX, 1, BLOCK), jnp.int32),
+            jax.ShapeDtypeStruct((QTOTAL, 1, BLOCK), jnp.int32),
+            jax.ShapeDtypeStruct((QTOTAL - NEAR_BLOCKS, 1, BLOCK), jnp.int32),
         ),
         in_specs=[smem, vmem],
-        out_specs=(smem, vmem),
+        out_specs=(smem, vmem, vmem, vmem),
         name="plan",
     )(quotas, neg_rows)
 
 
 def kernel(
     matching, plan, table, state, src_table_hbm, src_state, relation,
-    src_ids, dst_ids, rel_ids, slots,
+    src_ids, dst_ids, rel_ids, slots, near_ids, far_ids,
     src_step_out, src_state_out, part_out, dst_step_out, dst_state_out, rel_out,
-    shards, low, own, landed_high, landed_low, picked, states, src_table,
+    shards, far, low, own, landed_a, landed_b, landed_low, picked_a, picked_b, picked_low,
+    states, src_table,
     table2, part2, rel2, query_b, hold, coefs, negs, negs_t, neg_grad, spread,
     src_acc, dst_acc, rel_acc, taken, got_right, got_left,
     rel_mine, rel_rows, rel_sums,
@@ -164,7 +173,6 @@
     sibling = z * 2 + 1 - core
     others = [(p + k) % N_DOM for k in range(1, N_DOM)]
     edge_others = [(e + k) % N_EDGE for k in range(1, N_EDGE)]
-    rows_p, cols_p = piece(p)
     sent = []
 
     fetch = pltpu.make_async_copy(src_table_hbm, src_table, local_sem.at[0])
@@ -175,45 +183,49 @@
 
     greet([(t, e) for t in others] + [(p, t) for t in edge_others])
 
-    landed = (landed_high, landed_low)
+    landed = (landed_a, landed_b, landed_low)
+    picked = (picked_a, picked_b, picked_low)
 
     def spread_pieces(part):
         copies = []
         for k, t in enumerate(others):
-            rows, cols = piece(t)
+            rows, cols = piece(t, part)
             copy = remote(
-                own.at[part, rows, cols], landed[part].at[p],
+                own.at[PAIRED[part][0], rows, cols], landed[part].at[p],
                 own_send.at[part, k], own_recv.at[part, k], t, e,
             )
             copy.start()
             copies.append(copy)
-        landed[part][p] = own[part, rows_p, cols_p]
+        rows, cols = piece(p, part)
+        landed[part][p] = own[PAIRED[part][0], rows, cols]
         sent.extend(copies)
         return copies
 
     def pick(part, came, target_ref):
         for copy in came:
             copy.wait_recv()
+        rows, cols = piece(p, part)
         copies = []
         for k, t in enumerate(others):
-            picked[part, k] = landed[part][matching[t]]
+            picked[part][k] = landed[part][matching[t]]
             copy = remote(
-                picked.at[part, k], target_ref.at[rows_p, cols_p],
+                picked[part].at[k], target_ref.at[rows, cols],
                 pick_send.at[part, k], pick_recv.at[part, k], t, e,
             )
             copy.start()
             copies.append(copy)
-        target_ref[rows_p, cols_p] = landed[part][matching[p]]
+        target_ref[rows, cols] = landed[part][matching[p]]
         sent.extend(copies)
         return copies
 
-    came_high = spread_pieces(0)
-
+    came_a = spread_pieces(0)
     rel_acc[...] = jnp.zeros_like(rel_acc)
     src_acc[...] = jnp.zeros_like(src_acc)
     dst_acc[...] = jnp.zeros_like(dst_acc)
+    rel2[:DIM], rel2[DIM:] = split(relation[...].T)
+    picks_a = pick(0, came_a, shards.at[e])
+    came_b = spread_pieces(1)
     neg_grad[...] = jnp.zeros_like(neg_grad)
-    rel2[:DIM], rel2[DIM:] = split(relation[...].T)
     fetch.wait()
     table2[:DIM], table2[DIM:] = split(src_table[...])
 
@@ -253,20 +265,16 @@
             hold[:HALF, cols] = pos_coef * d_re
             hold[HALF:, cols] = pos_coef * d_im
 
-    came_high = pick(0, came_high, shards.at[e])
-    queries(0, 2)
-    for copy in came_high:
-        copy.wait_recv()
-
     flying = {}
 
     def go(step, half, to_right):
         source = ((z - step + N_Z) % N_Z if to_right else (z + step) % N_Z) * 2 + core
         start, size = CUT[half]
         ref = shards.at[source, pl.ds(start, size)]
+        target = far.at[core, pl.ds(start, size)] if step == FAR - 1 else ref
         sems = (right_send, right_recv) if to_right else (left_send, left_recv)
         copy = remote(
-            ref, ref, sems[0].at[step, half], sems[1].at[step, half],
+            ref, target, sems[0].at[step, half], sems[1].at[step, half],
             p, right if to_right else left,
         )
         copy.start()
@@ -277,7 +285,8 @@
 
     def cross(slot, source_z, half):
         start, size = CUT[half]
-        ref = shards.at[source_z * 2 + core, pl.ds(start, size)]
+        held, at = (far, core) if slot == 2 * FAR - 1 else (shards, source_z * 2 + core)
+        ref = held.at[at, pl.ds(start, size)]
         copy = remote(ref, ref, core_send.at[slot, half], core_recv.at[slot, half], p, sibling)
         copy.start()
         across.append(copy)
@@ -296,52 +305,54 @@
                 slot = 2 * step - 1 if to_right else 2 * step
             cross(slot, source_z, half)
 
-    for half in range(2):
+    def begin(half, picks):
+        for copy in picks:
+            copy.wait_recv()
         go(0, half, True)
         go(0, half, False)
-    for half in range(2):
         cross(0, z, half)
-    came_low = spread_pieces(1)
+
+    begin(0, picks_a)
+    picks_b = pick(1, came_b, shards.at[e])
+    queries(0, 2)
+    begin(1, picks_b)
+    came_low = spread_pieces(2)
     state_copies = []
     for k, t in enumerate(others):
         copy = remote(states.at[p], states.at[p], state_send.at[k], state_recv.at[k], t, e)
         copy.start()
         state_copies.append(copy)
     sent.extend(state_copies)
-
+    forward(1, 0)
     queries(2, 5)
-    came_low = pick(1, came_low, low)
-    forward(1, 0)
+    picks_low = pick(2, came_low, low)
+    forward(1, 1)
     queries(5, 8)
-    forward(1, 1)
+    forward(2, 0)
     part2[:DIM] = shards[e, :DIM]
-    for copy in came_low:
+    for copy in picks_low:
         copy.wait_recv()
     part2[DIM:] = low[:DIM]
     part_done = pltpu.make_async_copy(part2, part_out, local_sem.at[1])
     part_done.start()
     positives(0, 2)
-    forward(2, 0)
-    positives(2, 4)
     forward(2, 1)
-    positives(4, 6)
+    positives(2, 5)
     forward(3, 0)
-    positives(6, 7)
+    positives(5, 8)
     forward(3, 1)
-    positives(7, 8)
-    forward(4, 0)
-    forward(4, 1)
-    for copy in across:
-        copy.wait()
-
-    for j in range(QTOTAL):
-        hot = onehot(slots[plan[QTOTAL + j]], ROWS)
+
+    def gather(j):
+        hot = onehot(near_ids[j], ROWS)
         found = jnp.dot(shards[plan[j], :DIM], hot, preferred_element_type=F32)
+        if j >= NEAR_BLOCKS:
+            hot = onehot(far_ids[j - NEAR_BLOCKS], ROWS)
+            found += jnp.dot(far[plan[QTOTAL + j]], hot, preferred_element_type=F32)
         negs[:, j * BLOCK : (j + 1) * BLOCK] = found.astype(BF16)
         negs_t[j * BLOCK : (j + 1) * BLOCK, :] = found.T.astype(BF16)
 
-    def negatives(first, last):
-        @pl.loop(0, N_CHUNK)
+    def negatives(first, last, chunk_from=0, chunk_to=N_CHUNK):
+        @pl.loop(chunk_from, chunk_to)
         def _(i):
             cols = chunk_cols(i)
             scores = jnp.dot(
@@ -356,6 +367,20 @@
                 at = j * BLOCK - first
                 neg_grad[j] += added[:, at : at + BLOCK]
 
+    for copy in across:
+        copy.wait()
+    across.clear()
+    for j in range(NEAR_BLOCKS):
+        gather(j)
+    negatives(0, 512, 0, 4)
+    forward(4, 0)
+    forward(4, 1)
+    negatives(0, 512, 4, 8)
+    for copy in across:
+        copy.wait()
+    for j in range(NEAR_BLOCKS, QTOTAL):
+        gather(j)
+
     for copy in sent:
         copy.wait_send()
     sent.clear()
@@ -373,6 +398,7 @@
         return summed + lax.dot_general(low_part, hot, BY_COLS, preferred_element_type=F32)
 
     def contribute(at):
+        at = N_Z - 1 - at
         d = DISTANCES[at]
         shards[N_Z + d, :DIM] = dense(2 * at + 1).astype(BF16)
         copy = remote(
@@ -387,11 +413,11 @@
     joined = set()
     ring = {}
 
-    def reduce_step(step, half):
+    def reduce_step(step, half, ways=(True, False)):
         d = FAR - step
         start, size = CUT[half]
         rows = pl.ds(start, size)
-        for to_right in (True, False):
+        for to_right in ways:
             if step == 0 and to_right != (half == 0):
                 continue
             place = d if to_right else (N_Z - d) % N_Z
@@ -430,15 +456,16 @@
                 spread[...], rel_hot, BY_COLS, preferred_element_type=F32
             )
 
-    negatives(0, NEAR_FROM)
+    negatives(1024, 1536)
     contribute(0)
     reduce_step(0, 0)
     reduce_step(0, 1)
-    negatives(NEAR_FROM, NNEG)
+    negatives(512, 1024)
     contribute(1)
     contribute(2)
-    reduce_step(1, 0)
-    reduce_step(1, 1)
+    for way in (True, False):
+        for half in range(2):
+            reduce_step(1, half, (way,))
     contribute(3)
     contribute(4)
     query_grads(0, 2)
@@ -538,15 +565,15 @@
             jax.ShapeDtypeStruct((1, ROWS), F32),
             jax.ShapeDtypeStruct((NREL, 1, DIM), F32),
         ),
-        in_specs=[smem, smem, vmem, vmem, hbm] + [vmem] * 6,
+        in_specs=[smem, smem, vmem, vmem, hbm] + [vmem] * 8,
         out_specs=(hbm, vmem, hbm, hbm, vmem, vmem),
         scratch_shapes=[
             VMEM((N_EDGE, PAD_DIM, ROWS), BF16),
+            VMEM((2, DIM, ROWS), BF16),
             VMEM((PAD_DIM, ROWS), BF16),
             VMEM((2, PAD_DIM, ROWS), BF16),
-            VMEM((N_DOM, PIECE_ROWS, PIECE_COLS), BF16),
-            VMEM((N_DOM, PIECE_ROWS, PIECE_COLS), BF16),
-            VMEM((2, N_DOM - 1, PIECE_ROWS, PIECE_COLS), BF16),
+            *(VMEM((N_DOM, size, PIECE_COLS), BF16) for _, _, size in PAIRED),
+            *(VMEM((N_DOM - 1, size, PIECE_COLS), BF16) for _, _, size in PAIRED),
             VMEM((N_DOM, 1, ROWS), F32),
             VMEM((DIM, ROWS), F32),
             VMEM((2 * DIM, ROWS), BF16),
@@ -568,8 +595,8 @@
             VMEM((NREL, 1, DIM), F32),
             VMEM((N_DOM, 1, DIM), F32),
             VMEM((N_EDGE, 1, DIM), F32),
-            dma((2, N_DOM - 1)), dma((2, N_DOM - 1)),
-            dma((2, N_DOM - 1)), dma((2, N_DOM - 1)),
+            dma((3, N_DOM - 1)), dma((3, N_DOM - 1)),
+            dma((3, N_DOM - 1)), dma((3, N_DOM - 1)),
             dma((N_DOM - 1,)), dma((N_DOM - 1,)),
             dma((FAR, 2)), dma((FAR, 2)), dma((FAR, 2)), dma((FAR, 2)),
             dma((N_Z, 2)), dma((N_Z, 2)),
@@ -585,6 +612,36 @@
     )(*args)
 
 
+def finish_kernel(
+    src_table, src_step, src_state, part, dst_step, dst_state, relation, rel_total,
+    src_out, src_state_out, dst_out, dst_state_out, relation_out,
+):
+    src_out[...] = src_table[...] - src_step[...]
+    src_state_out[...] = src_state[...]
+    dst_out[...] = part[:DIM].astype(F32) + part[DIM:].astype(F32) - dst_step[...]
+    dst_state_out[...] = dst_state[...]
+    for r in range(NREL):
+        relation_out[r : r + 1] = relation[r : r + 1] - rel_rate * rel_total[r]
+
+
+def finish(*args):
+    vmem = pl.BlockSpec(memory_space=VMEM)
+    return pl.pallas_call(
+        finish_kernel,
+        out_shape=(
+            jax.ShapeDtypeStruct((DIM, ROWS), F32),
+            jax.ShapeDtypeStruct((1, ROWS), F32),
+            jax.ShapeDtypeStruct((DIM, ROWS), F32),
+            jax.ShapeDtypeStruct((1, ROWS), F32),
+            jax.ShapeDtypeStruct((NREL, DIM), F32),
+        ),
+        in_specs=[vmem] * 8,
+        out_specs=(vmem,) * 5,
+        compiler_params=pltpu.CompilerParams(vmem_limit_bytes=60 * 2**20),
+        name="finish",
+    )(*args)
+
+
 def shards(
     src_table,
     src_state,
@@ -598,7 +655,7 @@
     neg_rows,
     quotas,
 ):
-    plan, slots = make_plan(quotas, neg_rows.reshape(N_EDGE, QMAX * BLOCK))
+    plan, slots, near_ids, far_ids = make_plan(quotas, neg_rows.reshape(N_EDGE, QMAX * BLOCK))
     src_step, src_state_out, part, dst_step, dst_state_out, rel_total = run(
         matching,
         plan,
@@ -611,13 +668,18 @@
         edge_dst.reshape(1, EDGES),
         edge_rel.reshape(1, EDGES),
         slots,
+        near_ids,
+        far_ids,
+    )
+    src_out, src_state_out, dst_out, dst_state_out, relation_out = finish(
+        src_table, src_step, src_state_out, part, dst_step, dst_state_out, relation.T, rel_total
     )
     return (
-        src_table - src_step,
+        src_out,
         src_state_out.reshape(ROWS),
-        part[:DIM].astype(F32) + part[DIM:].astype(F32) - dst_step,
+        dst_out,
         dst_state_out.reshape(ROWS),
-        relation - rel_rate * rel_total.reshape(NREL, DIM).T,
+        relation_out.T,
     )
 
 

time: 138 us -> 134 us (0.971)
  other arithmetic: 4.01 us -> 0 us
  Pallas kernels: 131 us -> 133 us
  local copies, waits for them, and re-layouts: 2 us -> 0 us
    sub x3 -> x0, other arithmetic: 3.98 us -> none  [the longest x1 2.3 us: shards(): src_table - src_step]
    pallas_call x0 -> x1, Pallas kernels: none -> 3.15 us  [finish(): pl.pallas_call(finish_kernel, out_shape=(jax.ShapeDtypeStruct((DIM, ROWS)...]
    unnamed x16 -> x0, local copies, waits for them, and re-layouts: 2 us -> none
where the time goes in v3:
time: 134 us
  Pallas kernels  133 us (99%)
    pallas_call x1, Pallas kernels, run(): pl.pallas_call(kernel, out_shape=(jax.ShapeDtypeStruct((DIM, ROWS), F32),...  128 us
    pallas_call x1, Pallas kernels, finish(): pl.pallas_call(finish_kernel, out_shape=(jax.ShapeDtypeStruct((DIM, ROWS)...  3.15 us

profile of v3, /device:TPU:1, one launch (start us, length us, event | category | flops | bytes accessed | tf_op | source)
XLA Modules:
  0.0 133.9 jit_solution(17540219128570613541)
XLA Ops:
  0.6 1.8 %plan.1 = (s32[40]{0:T(128)}, s32[32,1,128]{2,1,0:T(1,128)}, s32[12,1,128]{2,1,0:T(1,128)}, s32[4,1,128]{2,1,0:T(1,128)}) custom-call(s32[1,16]{1,0:T(1,128)} %quotas.1, s32[16,256]{1,0:T(8,128)} %bitcast.15), custom_call_target="tpu_custom_call" | custom-call | tf_op jit(solution)/shard_map/plan/pallas_call | solution.py:140
  2.4 128.3 %bucket_step.1 = (f32[400,512]{1,0:T(8,128)}, f32[1,512]{1,0:T(1,128)}, bf16[800,512]{1,0:T(8,128)(2,1)}, f32[400,512]{1,0:T(8,128)}, f32[1,512]{1,0:T(1,128)}, /*index=5*/f32[16,1,400]{2,1,0:T(1,128)}) custom-call(s32[16]{0:T(128)} %matching.1, s32[40]{0:T(128)} %get-tuple-element.20.plan, f32[400,512]{1,0:T(8,128)} %table.1, f32[1,512]{1,0:T(1,128)} %bitcast.16, ...), custom_call_target="tpu_custom_call" | custom-call | tf_op jit(solution)/shard_map/bucket_step/pallas_call | solution.py:558
  130.7 3.2 %finish.1 = (f32[400,512]{1,0:T(8,128)}, f32[1,512]{1,0:T(1,128)}, f32[400,512]{1,0:T(8,128)}, f32[1,512]{1,0:T(1,128)}, f32[16,400]{1,0:T(8,128)}) custom-call(f32[400,512]{1,0:T(8,128)} %src_table.1, f32[400,512]{1,0:T(8,128)} %get-tuple-element.24.src_step, f32[1,512]{1,0:T(1,128)} %get-tuple-element.25.src_state, ...), custom_call_target="tpu_custom_call" | custom-call | tf_op jit(solution)/shard_map/finish/pallas_call | solution.py:629

commit v4 on v3

--- a/solution.py
+++ b/solution.py
@@ -22,6 +22,7 @@
 FAR = N_Z // 2
 DISTANCES = (0, 7, 1, 6, 2, 5, 3, 4)
 NEAR_BLOCKS = 8
+EARLY = 512
 
 PAIRED = ((0, 0, 48), (0, 192, 64), (1, 0, 112))
 PIECE_COLS = 128
@@ -156,7 +157,7 @@
     src_ids, dst_ids, rel_ids, slots, near_ids, far_ids,
     src_step_out, src_state_out, part_out, dst_step_out, dst_state_out, rel_out,
     shards, far, low, own, landed_a, landed_b, landed_low, picked_a, picked_b, picked_low,
-    states, src_table,
+    states, source,
     table2, part2, rel2, query_b, hold, coefs, negs, negs_t, neg_grad, spread,
     src_acc, dst_acc, rel_acc, taken, got_right, got_left,
     rel_mine, rel_rows, rel_sums,
@@ -175,7 +176,7 @@
     edge_others = [(e + k) % N_EDGE for k in range(1, N_EDGE)]
     sent = []
 
-    fetch = pltpu.make_async_copy(src_table_hbm, src_table, local_sem.at[0])
+    fetch = pltpu.make_async_copy(src_table_hbm, src_acc.at[pl.ds(0, DIM)], local_sem.at[0])
     fetch.start()
     own[0, :DIM], own[1, :DIM] = split(table[...])
     own[:, DIM:] = jnp.zeros((2, PAD_DIM - DIM, ROWS), BF16)
@@ -220,30 +221,32 @@
 
     came_a = spread_pieces(0)
     rel_acc[...] = jnp.zeros_like(rel_acc)
-    src_acc[...] = jnp.zeros_like(src_acc)
     dst_acc[...] = jnp.zeros_like(dst_acc)
     rel2[:DIM], rel2[DIM:] = split(relation[...].T)
     picks_a = pick(0, came_a, shards.at[e])
     came_b = spread_pieces(1)
     neg_grad[...] = jnp.zeros_like(neg_grad)
     fetch.wait()
-    table2[:DIM], table2[DIM:] = split(src_table[...])
+    table2[:DIM], table2[DIM:] = split(src_acc[:DIM])
+    src_acc[...] = jnp.zeros_like(src_acc)
 
     def chunk_cols(i):
         return pl.ds(pl.multiple_of(i * CHUNK, CHUNK), CHUNK)
 
-    def source_rows(cols):
-        src_hot = onehot(src_ids[:, cols], ROWS)
+    def relation_rows(cols):
         rel_hot = onehot(rel_ids[:, cols], NREL)
-        s_re, s_im = both(jnp.dot(table2[...], src_hot, preferred_element_type=F32))
         r_re, r_im = both(jnp.dot(rel2[...], rel_hot, preferred_element_type=F32))
-        return src_hot, rel_hot, s_re, s_im, r_re, r_im
+        return rel_hot, r_re, r_im
 
     def queries(first, last):
         @pl.loop(first, last)
         def _(i):
             cols = chunk_cols(i)
-            _, _, s_re, s_im, r_re, r_im = source_rows(cols)
+            src_hot = onehot(src_ids[:, cols], ROWS)
+            s_re, s_im = both(jnp.dot(table2[...], src_hot, preferred_element_type=F32))
+            _, r_re, r_im = relation_rows(cols)
+            source[:HALF, cols] = s_re
+            source[HALF:, cols] = s_im
             q_re, q_im = product(s_re, s_im, r_re, r_im)
             hold[:HALF, cols] = q_re
             hold[HALF:, cols] = q_im
@@ -340,6 +343,7 @@
     positives(2, 5)
     forward(3, 0)
     positives(5, 8)
+    dst_acc[:DIM] = dst_acc[:DIM] + dst_acc[DIM:]
     forward(3, 1)
 
     def gather(j):
@@ -359,7 +363,12 @@
                 negs_t[first:last], query_b[:, cols], preferred_element_type=F32
             )
             coef = (0.5 * weight + 0.5 * weight * jnp.tanh(0.5 * scores)).astype(BF16)
-            coefs[first:last, cols] = coef
+            if first < EARLY:
+                hold[:, cols] += jnp.dot(
+                    negs[:, first:last], coef, preferred_element_type=F32
+                )
+            else:
+                coefs[first - EARLY : last - EARLY, cols] = coef
             added = lax.dot_general(
                 query_b[:, cols], coef, BY_COLS, preferred_element_type=F32
             )
@@ -372,10 +381,10 @@
     across.clear()
     for j in range(NEAR_BLOCKS):
         gather(j)
-    negatives(0, 512, 0, 4)
+    negatives(0, EARLY, 0, 4)
     forward(4, 0)
     forward(4, 1)
-    negatives(0, 512, 4, 8)
+    negatives(0, EARLY, 4, 8)
     for copy in across:
         copy.wait()
     for j in range(NEAR_BLOCKS, QTOTAL):
@@ -393,9 +402,9 @@
         parts = jnp.concatenate([neg_grad[first + b] for b in range(QMAX)], axis=1)
         ids = jnp.concatenate([slots[owner * QMAX + b] for b in range(QMAX)], axis=1)
         hot = onehot(ids, ROWS)
-        high, low_part = split(parts)
-        summed = lax.dot_general(high, hot, BY_COLS, preferred_element_type=F32)
-        return summed + lax.dot_general(low_part, hot, BY_COLS, preferred_element_type=F32)
+        stacked = jnp.concatenate(split(parts), axis=0)
+        summed = lax.dot_general(stacked, hot, BY_COLS, preferred_element_type=F32)
+        return summed[:DIM] + summed[DIM:]
 
     def contribute(at):
         at = N_Z - 1 - at
@@ -443,8 +452,10 @@
         @pl.loop(first, last)
         def _(i):
             cols = chunk_cols(i)
-            src_hot, rel_hot, s_re, s_im, r_re, r_im = source_rows(cols)
-            g = jnp.dot(negs[...], coefs[:, cols], preferred_element_type=F32)
+            src_hot = onehot(src_ids[:, cols], ROWS)
+            rel_hot, r_re, r_im = relation_rows(cols)
+            s_re, s_im = source[:HALF, cols], source[HALF:, cols]
+            g = jnp.dot(negs[:, EARLY:], coefs[:, cols], preferred_element_type=F32)
             g_re = hold[:HALF, cols] + g[:HALF]
             g_im = hold[HALF:, cols] + g[HALF:]
             put_split(spread, *back(g_re, g_im, r_re, r_im))
@@ -468,18 +479,17 @@
             reduce_step(1, half, (way,))
     contribute(3)
     contribute(4)
-    query_grads(0, 2)
+    query_grads(0, 3)
     reduce_step(2, 0)
-    query_grads(2, 3)
+    query_grads(3, 4)
     contribute(5)
     contribute(6)
     reduce_step(2, 1)
-    query_grads(3, 5)
+    query_grads(4, 7)
     contribute(7)
     reduce_step(3, 0)
-    query_grads(5, 7)
+    query_grads(7, 8)
     reduce_step(3, 1)
-    query_grads(7, 8)
 
     rel_grad = (rel_acc[:DIM] + rel_acc[DIM:]).T
     for r in range(NREL):
@@ -511,7 +521,6 @@
         copy.start()
         second_copies.append(copy)
 
-    dst_acc[:DIM] = dst_acc[:DIM] + dst_acc[DIM:]
     for copy in state_copies:
         copy.wait_recv()
     part_state = states[matching[p]]
@@ -575,13 +584,13 @@
             *(VMEM((N_DOM, size, PIECE_COLS), BF16) for _, _, size in PAIRED),
             *(VMEM((N_DOM - 1, size, PIECE_COLS), BF16) for _, _, size in PAIRED),
             VMEM((N_DOM, 1, ROWS), F32),
-            VMEM((DIM, ROWS), F32),
+            VMEM((DIM, EDGES), F32),
             VMEM((2 * DIM, ROWS), BF16),
             VMEM((2 * DIM, ROWS), BF16),
             VMEM((2 * DIM, NREL), BF16),
             VMEM((DIM, EDGES), BF16),
             VMEM((DIM, EDGES), F32),
-            VMEM((NNEG, EDGES), BF16),
+            VMEM((NNEG - EARLY, EDGES), BF16),
             VMEM((DIM, NNEG), BF16),
             VMEM((NNEG, DIM), BF16),
             VMEM((QTOTAL + QMAX, DIM, BLOCK), F32),

time: 134 us -> 132 us (0.985)
  Pallas kernels: 133 us -> 131 us
    pallas_call x1, Pallas kernels: 128 us -> 126 us  [run(): pl.pallas_call(kernel, out_shape=(jax.ShapeDtypeStruct((DIM, ROWS), F32),...]
where the time goes in v4:
time: 132 us; the launch traced here: 131 us
  Pallas kernels  131 us (99%)
    pallas_call x1, Pallas kernels, run(): pl.pallas_call(kernel, out_shape=(jax.ShapeDtypeStruct((DIM, ROWS), F32),...  126 us
    pallas_call x1, Pallas kernels, finish(): pl.pallas_call(finish_kernel, out_shape=(jax.ShapeDtypeStruct((DIM, ROWS)...  3.15 us

profile of v4, /device:TPU:1, one launch (start us, length us, event | category | flops | bytes accessed | tf_op | source)
XLA Modules:
  0.0 131.4 jit_solution(13061486138188715335)
XLA Ops:
  0.6 1.8 %plan.1 = (s32[40]{0:T(128)}, s32[32,1,128]{2,1,0:T(1,128)}, s32[12,1,128]{2,1,0:T(1,128)}, s32[4,1,128]{2,1,0:T(1,128)}) custom-call(s32[1,16]{1,0:T(1,128)} %quotas.1, s32[16,256]{1,0:T(8,128)} %bitcast.15), custom_call_target="tpu_custom_call" | custom-call | tf_op jit(solution)/shard_map/plan/pallas_call | solution.py:141
  2.4 125.8 %bucket_step.1 = (f32[400,512]{1,0:T(8,128)}, f32[1,512]{1,0:T(1,128)}, bf16[800,512]{1,0:T(8,128)(2,1)}, f32[400,512]{1,0:T(8,128)}, f32[1,512]{1,0:T(1,128)}, /*index=5*/f32[16,1,400]{2,1,0:T(1,128)}) custom-call(s32[16]{0:T(128)} %matching.1, s32[40]{0:T(128)} %get-tuple-element.20.plan, f32[400,512]{1,0:T(8,128)} %table.1, f32[1,512]{1,0:T(1,128)} %bitcast.16, ...), custom_call_target="tpu_custom_call" | custom-call | tf_op jit(solution)/shard_map/bucket_step/pallas_call | solution.py:567
  128.2 3.2 %finish.1 = (f32[400,512]{1,0:T(8,128)}, f32[1,512]{1,0:T(1,128)}, f32[400,512]{1,0:T(8,128)}, f32[1,512]{1,0:T(1,128)}, f32[16,400]{1,0:T(8,128)}) custom-call(f32[400,512]{1,0:T(8,128)} %src_table.1, f32[400,512]{1,0:T(8,128)} %get-tuple-element.24.src_step, f32[1,512]{1,0:T(1,128)} %get-tuple-element.25.src_state, ...), custom_call_target="tpu_custom_call" | custom-call | tf_op jit(solution)/shard_map/finish/pallas_call | solution.py:638
